TPU v7x, 32 devices: a whole 2x2x4 slice. The times are simulated.
32 devices in a mesh: grp: 4 (over y, x), dp: 8 (over z, core).
Axes of the slice: x: 2, y: 2, z: 4, core: 2. Of those that a mesh axis runs over, the one named last changes fastest.
Arguments:
- tokens: bfloat16 [32, 1024, 1024], P(('grp', 'dp')), may hold values from -12 to 12
- cotangent: bfloat16 [32, 1024, 1024], P(('grp', 'dp')), may hold values from -6 to 6
- segment_ids: int32 [32, 1024], P(('grp', 'dp')), may hold values from 0 to 15, never falling along the last dimension, each value on 1 to 512 neighbouring positions
- in_weight: float32 [1024, 4384], P('grp'), may hold values from -0.1875 to 0.1875
- out_weight: float32 [2048, 1024], P('grp'), may hold values from -0.125 to 0.125
- filter_weight: float32 [4, 2304], P(None, 'grp'), may hold values from -3 to 3
- vectors: float32 [5472], P('grp'), may hold values from -7 to 3
- in_first: float32 [1024, 4384], P('grp'), may hold values from -512 to 512
- out_first: float32 [2048, 1024], P('grp'), may hold values from -1024 to 1024
- filter_first: float32 [4, 2304], P(None, 'grp'), may hold values from -320 to 320
- vector_first: float32 [5472], P('grp'), may hold values from -1024 to 1024
- in_second: float32 [1024, 4384], P('grp'), may hold values from 8192 to 32768
- out_second: float32 [2048, 1024], P('grp'), may hold values from 32768 to 131072
- filter_second: float32 [4, 2304], P(None, 'grp'), may hold values from 3276 to 13107
- vector_second: float32 [5472], P('grp'), may hold values from 32768 to 131072
Outputs:
- block_out: bfloat16 [32, 1024, 1024], P(('grp', 'dp'))
- token_grad: float32 [32, 1024, 1024], P(('grp', 'dp'))
- in_new: float32 [1024, 4384], P('grp')
- out_new: float32 [2048, 1024], P('grp')
- filter_new: float32 [4, 2304], P(None, 'grp')
- vectors_new: float32 [5472], P('grp')
- in_first_new: float32 [1024, 4384], P('grp')
- out_first_new: float32 [2048, 1024], P('grp')
- filter_first_new: float32 [4, 2304], P(None, 'grp')
- vector_first_new: float32 [5472], P('grp')
- in_second_new: float32 [1024, 4384], P('grp')
- out_second_new: float32 [2048, 1024], P('grp')
- filter_second_new: float32 [4, 2304], P(None, 'grp')
- vector_second_new: float32 [5472], P('grp')
Inputs may be any that keep to these rules, and one draw needn't show every extreme that they name: `segment_ids`: along each row the ids never fall and every id appears; some document of each row has exactly 512 tokens.
All inputs are finite; a program needn't handle non-finite values.
Results may differ from a plain program's by a relative error of at most 0.012.
The roundings to bfloat16 on the way count: a program that leaves them out, or rounds other values in their place, can miss the bound.
Values may be sent and summed in bfloat16 or wider, within the bound.
A program may use at most 320 MiB of HBM per device.

v0:
```python
from functools import partial

import jax
import jax.numpy as jnp
from jax import lax
from jax.sharding import PartitionSpec as P

D = 1024
H = 32
P_SIZE = 64
NSTATE = 128
KERNEL = 4
BLOCK = 256
STEP = 7
D_INNER = 2048
CONV_CH = 2304


EPSILON = 1e-05
ADAM_EPSILON = 1e-08
BETA_FIRST = 0.5
BETA_SECOND = 0.5
WEIGHT_DECAY = 0.1


def state_scan(inputs, bmat, cmat, step_size, decay_rate, skip_gain, segment):
    highest = lax.Precision.HIGHEST
    length = inputs.shape[0]
    count = length // BLOCK
    x_blocks = inputs.reshape(count, BLOCK, H, P_SIZE)
    b_blocks = bmat.reshape(count, BLOCK, NSTATE)
    c_blocks = cmat.reshape(count, BLOCK, NSTATE)
    step_blocks = jnp.swapaxes(step_size.reshape(count, BLOCK, H), 1, 2)
    seg_blocks = segment.reshape(count, BLOCK)
    cumulative = jnp.cumsum(step_blocks * decay_rate[None, :, None], axis=2)
    positions = jnp.arange(BLOCK)
    same_mask = (seg_blocks[:, :, None] == seg_blocks[:, None, :]) & (
        positions[:, None] >= positions[None, :]
    )
    same_mask = same_mask[:, None]
    differences = cumulative[:, :, :, None] - cumulative[:, :, None, :]
    decay_matrix = jnp.where(same_mask, jnp.exp(jnp.where(same_mask, differences, 0.0)), 0.0)
    scores = jnp.einsum("ctn,csn->cts", c_blocks, b_blocks, precision=highest)
    weights = scores[:, None] * decay_matrix * step_blocks[:, :, None, :]
    inner_part = jnp.einsum("chts,cshp->cthp", weights, x_blocks, precision=highest)
    last_cumsum = cumulative[:, :, -1:]
    tail_weight = (
        jnp.exp(last_cumsum - cumulative)
        * step_blocks
        * (seg_blocks == seg_blocks[:, -1:]).astype(inputs.dtype)[:, None, :]
    )
    weighted_x = x_blocks * jnp.swapaxes(tail_weight, 1, 2)[..., None]
    local_state = jnp.einsum("cshp,csn->chpn", weighted_x, b_blocks, precision=highest)
    block_ends = seg_blocks[:, -1]
    before_ends = jnp.concatenate([jnp.full((1,), -1, jnp.int32), block_ends[:-1]])
    keep_state = (block_ends == before_ends).astype(inputs.dtype)
    fade_rate = jnp.exp(last_cumsum[:, :, 0]) * keep_state[:, None]

    def advance(carried_state, block_item):
        fade_now, local_now = block_item
        return (fade_now[:, None, None] * carried_state + local_now, carried_state)

    start_state = jnp.zeros((H, P_SIZE, NSTATE), inputs.dtype)
    unused_state, entering = lax.scan(advance, start_state, (fade_rate, local_state))
    reach_mask = (seg_blocks == before_ends[:, None]).astype(inputs.dtype)
    carried_part = jnp.einsum("ctn,chpn->cthp", c_blocks, entering, precision=highest)
    carried_part = (
        carried_part * (jnp.exp(jnp.swapaxes(cumulative, 1, 2)) * reach_mask[:, :, None])[..., None]
    )
    result = inner_part + carried_part + skip_gain[None, None, :, None] * x_blocks
    return result.reshape(length, H, P_SIZE)


def mixer(projected, filter_taps, vector_vals, segment):
    length = projected.shape[0]
    gate_in = projected[:, :D_INNER]
    conv_in = projected[:, D_INNER : D_INNER + CONV_CH]
    step_raw = projected[:, D_INNER + CONV_CH :]
    first_end = D + D_INNER
    bias_end = first_end + CONV_CH
    padded = jnp.concatenate([jnp.zeros((KERNEL - 1, CONV_CH), projected.dtype), conv_in], 0)
    seg_padded = jnp.concatenate([jnp.full((KERNEL - 1,), -1, jnp.int32), segment])
    filtered = jnp.zeros((length, CONV_CH), projected.dtype) + vector_vals[first_end:bias_end]
    for offset in range(KERNEL):
        shifted = padded[KERNEL - 1 - offset : KERNEL - 1 - offset + length]
        same_doc = (
            seg_padded[KERNEL - 1 - offset : KERNEL - 1 - offset + length] == segment
        ).astype(projected.dtype)
        filtered = filtered + shifted * same_doc[:, None] * filter_taps[offset]
    activated = jax.nn.silu(filtered)
    inputs = activated[:, :D_INNER].reshape(length, H, P_SIZE)
    bmat = activated[:, D_INNER : D_INNER + NSTATE]
    cmat = activated[:, D_INNER + NSTATE :]
    step_size = jax.nn.softplus(step_raw + vector_vals[bias_end : bias_end + H])
    decay_rate = -jnp.exp(vector_vals[bias_end + H : bias_end + 2 * H])
    skip_gain = vector_vals[bias_end + 2 * H :]
    scanned = state_scan(inputs, bmat, cmat, step_size, decay_rate, skip_gain, segment).reshape(
        length, D_INNER
    )
    gated = scanned * jax.nn.silu(gate_in)
    return (
        gated
        * lax.rsqrt(jnp.mean(gated * gated, -1, keepdims=True) + EPSILON)
        * vector_vals[D:first_end]
    )


def pre_norm(features, vector_vals):
    return (
        features
        * lax.rsqrt(jnp.mean(features * features, -1, keepdims=True) + EPSILON)
        * vector_vals[:D]
    )


def adam_step(master, first, second, grad, rate):
    first_new = BETA_FIRST * first + (1.0 - BETA_FIRST) * grad
    second_new = BETA_SECOND * second + (1.0 - BETA_SECOND) * grad * grad
    first_fix = 1.0 - BETA_FIRST**STEP
    second_fix = 1.0 - BETA_SECOND**STEP
    master_new = master - rate * (
        first_new / first_fix / (jnp.sqrt(second_new / second_fix) + ADAM_EPSILON)
        + WEIGHT_DECAY * master
    )
    return (master_new, first_new, second_new)


def contract_rows(left, right):
    return lax.dot_general(
        left, right, (((0,), (0,)), ((), ())), preferred_element_type=jnp.float32
    )


def contract_cols(left, right):
    return lax.dot_general(
        left, right, (((1,), (1,)), ((), ())), preferred_element_type=jnp.float32
    )


def local(
    tokens,
    cotangent,
    segment_ids,
    in_weight,
    out_weight,
    filter_weight,
    vectors,
    in_first,
    out_first,
    filter_first,
    vector_first,
    in_second,
    out_second,
    filter_second,
    vector_second,
):
    in_full, out_full, filter_full, vector_full = (
        lax.all_gather(in_weight.astype(jnp.bfloat16), "grp", axis=0, tiled=True),
        lax.all_gather(out_weight.astype(jnp.bfloat16), "grp", axis=0, tiled=True),
        lax.all_gather(filter_weight.astype(jnp.bfloat16), "grp", axis=1, tiled=True),
        lax.all_gather(vectors.astype(jnp.bfloat16), "grp", axis=0, tiled=True),
    )
    filter_taps = filter_full.astype(jnp.float32)
    vector_vals = vector_full.astype(jnp.float32)
    features = tokens[0].astype(jnp.float32)
    segment = segment_ids[0]
    normed, norm_back = jax.vjp(pre_norm, features, vector_vals)
    normed_low = normed.astype(jnp.bfloat16)
    projected = jnp.dot(normed_low, in_full, preferred_element_type=jnp.float32)
    mixed, mixer_back = jax.vjp(
        partial(mixer, segment=segment), projected, filter_taps, vector_vals
    )
    mixed_low = mixed.astype(jnp.bfloat16)
    branch_out = jnp.dot(mixed_low, out_full, preferred_element_type=jnp.float32)
    block_out = (features + branch_out).astype(jnp.bfloat16)
    grad_low = cotangent[0]
    grad_out = contract_rows(mixed_low, grad_low)
    grad_mixed = contract_cols(grad_low, out_full)
    grad_proj, grad_taps, grad_vec_mixer = mixer_back(grad_mixed)
    grad_proj_low = grad_proj.astype(jnp.bfloat16)
    grad_in = contract_rows(normed_low, grad_proj_low)
    grad_normed = contract_cols(grad_proj_low, in_full)
    grad_features, grad_vec_norm = norm_back(grad_normed)
    token_grad = grad_features + grad_low.astype(jnp.float32)
    grad_vectors = grad_vec_mixer + grad_vec_norm
    masters = (in_weight, out_weight, filter_weight)
    firsts = (in_first, out_first, filter_first)
    seconds = (in_second, out_second, filter_second)
    rates = (0.03, 0.02, 0.3)
    in_share, out_share, filter_share, vector_share = (
        lax.psum_scatter(grad_in, "grp", scatter_dimension=0, tiled=True),
        lax.psum_scatter(grad_out, "grp", scatter_dimension=0, tiled=True),
        lax.psum_scatter(grad_taps, "grp", scatter_dimension=1, tiled=True),
        lax.psum_scatter(grad_vectors, "grp", scatter_dimension=0, tiled=True),
    )
    in_total, out_total, filter_total, vector_total = lax.psum(
        (in_share, out_share, filter_share, vector_share), "dp"
    )
    totals = (in_total, out_total, filter_total)
    results = [
        adam_step(
            masters[index_mat],
            firsts[index_mat],
            seconds[index_mat],
            totals[index_mat],
            rates[index_mat],
        )
        for index_mat in range(3)
    ]
    vectors_new, vector_first_new, vector_second_new = adam_step(
        vectors, vector_first, vector_second, vector_total, 0.3
    )
    return (
        block_out[None],
        token_grad[None],
        results[0][0],
        results[1][0],
        results[2][0],
        vectors_new,
        results[0][1],
        results[1][1],
        results[2][1],
        vector_first_new,
        results[0][2],
        results[1][2],
        results[2][2],
        vector_second_new,
    )


def solution(mesh):
    in_specs = (
        P(("grp", "dp"), None, None),
        P(("grp", "dp"), None, None),
        P(("grp", "dp"), None),
        P("grp", None),
        P("grp", None),
        P(None, "grp"),
        P("grp"),
        P("grp", None),
        P("grp", None),
        P(None, "grp"),
        P("grp"),
        P("grp", None),
        P("grp", None),
        P(None, "grp"),
        P("grp"),
    )
    out_specs = (
        P(("grp", "dp"), None, None),
        P(("grp", "dp"), None, None),
        P("grp", None),
        P("grp", None),
        P(None, "grp"),
        P("grp"),
        P("grp", None),
        P("grp", None),
        P(None, "grp"),
        P("grp"),
        P("grp", None),
        P("grp", None),
        P(None, "grp"),
        P("grp"),
    )
    return jax.shard_map(local, mesh=mesh, in_specs=in_specs, out_specs=out_specs, check_vma=False)
```

profile of v0, /device:TPU:1, one launch (start us, length us, event | category | flops | bytes accessed | tf_op | source)
XLA Modules:
  0.0 986.3 jit_solution(7852397106455465231)
XLA Ops:
  15.8 13.2 %all-reduce.23 = bf16[5472]{0:T(1024)(128)(2,1)S(1)} all-reduce(bf16[5472]{0:T(1024)(128)(2,1)S(1)} %dynamic-update-slice), channel_id=1, replica_groups=mesh['grp'=4,'dp'=8] {'grp'}, use_global_device_ids=true, to_apply=%add.23 | all-reduce | flops 5472 | bytes 21888
  40.3 65.8 %all-gather.4.cloned.1.call-done = bf16[1024,4384]{0,1:T(8,128)(2,1)} async-done(((bf16[256,4384]{0,1:T(8,128)(2,1)}), bf16[1024,4384]{0,1:T(8,128)(2,1)}) %all-gather.4.cloned.1.call-update) | async-done | bytes 8978448 | tf_op jit(solution)/shard_map/all_gather | solution.py:158
  106.1 15.7 %fusion.91 = f32[1024,4384]{0,1:T(8,128)} fusion(bf16[1024,4384]{0,1:T(8,128)(2,1)} %all-gather.4.cloned.1.call-done, bf16[1,1024,1024]{2,1,0:T(8,128)(2,1)S(1)} %copy-done.6, f32[1024]{0:T(1024)S(1)} %slice.123, f32[1024]{0:T(1024)S(1)} %fusion.119), kind=kOutput, calls=%fused_computation.133 | convolution fusion | flops 9198108672 | bytes 29040640 | tf_op jit(solution)/shard_map/dot_general | solution.py:169
  126.6 12.2 %fusion.29 = (f32[1024,2304]{0,1:T(8,128)}, f32[1024,2304]{0,1:T(8,128)}) fusion(f32[2304]{0:T(1024)S(1)} %get-tuple-element.255, f32[1024]{0:T(1024)S(1)} %get-tuple-element.328, f32[2304]{0:T(1024)S(1)} %get-tuple-element.256, f32[1024]{0:T(1024)S(1)} %get-tuple-element.327, f32[2304]{0:T(1024)S(1)} %get-tuple-element.257, ...), kind=kLoop, calls=%fused_computation.57 | loop fusion | flops 35389440 | bytes 28369920 | tf_op jit(solution)/shard_map/jvp(jit(silu))/mul | solution.py:90
  152.9 10.6 %reshape.275 = f32[4,256,32,64]{1,0,3,2:T(4,128)} reshape(f32[1024,2048]{0,1:T(8,128)} %slice.129) | data formatting | bytes 16777216 | tf_op jit(solution)/shard_map/jvp()/reshape;jvp()/reshape | solution.py:30
  163.8 13.0 %fusion.43 = f32[4,32,64,128]{3,2,1,0:T(8,128)} fusion(f32[4,256,128,1]{2,1,3,0:T(8,128)S(1)} %copy.218, f32[4,256,32,64]{1,0,3,2:T(4,128)} %reshape.275, f32[4,256,32]{1,2,0:T(8,128)S(1)} %get-tuple-element.321), kind=kOutput, calls=%fused_computation.87 | convolution fusion | flops 3223322624 | bytes 13238272 | tf_op jit(solution)/shard_map/jvp(cshp,csn->chpn)/dot_general | solution.py:53
  179.3 10.0 %while.34 = (s32[]{:T(128)}, f32[32,64,128]{2,1,0:T(8,128)S(1)}, f32[4,32,64,128]{3,2,1,0:T(8,128)}, f32[4,32,1,1]{1,3,2,0:T(1,128)S(1)}, f32[4,32]{1,0:T(4,128)...) while((s32[]{:T(128)}, f32[32,64,128]{2,1,0:T(8,128)S(1)}, ...), condition=%wide.region_4.5_spmd.clone, body=%wide.region_3.4_spmd.clone.sunk | while | flops 1048579 | bytes 5244408 | solution.py:64
  204.6 45.2 %fusion.35 = f32[4,256,32,64]{1,3,2,0:T(8,128)} fusion(f32[4,256,32,64]{1,3,2,0:T(8,128)S(1)} %fusion.140, f32[4,256,32,64]{1,0,3,2:T(4,128)} %reshape.275, f32[4,32,256]{2,1,0:T(8,128)S(1)} %bitcast.274, f32[4,32,256]{2,1,0:T(8,128)S(1)} %copy_bitcast_fusion, f32[4,256,256]{2,1,0:T(8,128)S(1)} %fusion.139, pred[4,256,256]{2,1,0:T(8,128)(4,1)S(1)} %copy-done.27, ...), kind=kOutput, calls=%fused_computation.66 | convolution fusion | flops 6492782592 | bytes 26869888 | tf_op jit(solution)/shard_map/jvp(chts,cshp->cthp)/dot_general | solution.py:45
  249.8 13.8 %copy.195 = f32[4,256,32,64]{1,0,3,2:T(4,128)} copy(f32[4,256,32,64]{1,3,2,0:T(8,128)} %fusion.35) | data formatting | bytes 16777216 | tf_op jit(solution)/shard_map/jvp()/add | solution.py:70
  287.9 11.6 %multiply_reduce_fusion.7 = (f32[2048]{0:T(1024)}, f32[1024]{0:T(1024)S(1)}, f32[1024,2048]{0,1:T(8,128)S(1)}) fusion(f32[1024,2048]{0,1:T(8,128)} %copy-done.4, f32[1024]{0:T(1024)S(1)} %fusion.120, f32[2048]{0:T(1024)S(1)} %copy-done.60, bf16[2048,1024]{1,0:T(8,128)(2,1)} %all-gather.6.cloned.1.call-done, bf16[1,1024,1024]{2,1,0:T(8,128)(2,1)} %param.20), kind=kOutput, calls=%fused_computation.73 | convolution fusion | flops 4307547136 | bytes 23093248 | tf_op jit(solution)/shard_map/dot_general | solution.py:135
  299.5 16.3 %multiply_reduce_fusion.6 = (f32[2048]{0:T(1024)}, f32[1024,2048]{0,1:T(8,128)}, f32[1024,2048]{0,1:T(8,128)}) fusion(f32[1024,2304]{0,1:T(8,128)} %get-tuple-element.307, f32[1024,4384]{0,1:T(8,128)} %fusion.91, f32[1024,2048]{0,1:T(8,128)S(1)} %copy-done.5, f32[1024]{0:T(1024)S(1)} %multiply_multiply_fusion.8, f32[1024]{0:T(1024)S(1)} %fusion.120, ...), kind=kLoop, calls=%fused_computation.72 | loop fusion | flops 39843840 | bytes 58744832 | tf_op jit(solution)/shard_map/transpose(jvp())/reduce_sum | solution.py:70
  315.8 10.5 %reshape.282 = f32[4,256,32,64]{1,0,3,2:T(4,128)} reshape(f32[1024,2048]{0,1:T(8,128)} %get-tuple-element.295) | data formatting | bytes 16777216 | tf_op jit(solution)/shard_map/transpose(jvp())/reshape;transpose(jvp())/reshape | solution.py:71
  326.3 13.1 %fusion.39 = f32[4,32,64,128]{3,2,1,0:T(8,128)} fusion(f32[4,256,128,1]{2,1,3,0:T(8,128)S(1)} %copy.219, f32[4,256,32,64]{1,0,3,2:T(4,128)} %reshape.282, f32[4,256,32]{1,2,0:T(8,128)S(1)} %get-tuple-element.320), kind=kOutput, calls=%fused_computation.83 | convolution fusion | flops 3223322624 | bytes 13238272 | tf_op jit(solution)/shard_map/transpose(jvp(ctn,chpn->cthp))/dot_general | solution.py:66
  341.9 11.9 %while.35 = (s32[]{:T(128)}, f32[32,64,128]{2,1,0:T(8,128)S(1)}, f32[4,32]{1,0:T(4,128)S(1)}, f32[4,32,64,128]{3,2,1,0:T(8,128)}, f32[4,32,64,128]{3,2,1,0:T(8,1...) while((s32[]{:T(128)}, f32[32,64,128]{2,1,0:T(8,128)S(1)}, ...), condition=%wide.region_9.10_spmd.clone, body=%wide.region_7.9_spmd.clone.sunk | while | flops 1572836 | bytes 6292372 | solution.py:64
  353.9 13.6 %multiply_reduce_fusion.9 = (f32[4,256,32]{1,2,0:T(8,128)}, f32[4,256,32,64]{1,3,2,0:T(8,128)S(1)}) fusion(f32[4,256,32,64]{1,0,3,2:T(4,128)} %reshape.275, f32[4,256,128,1]{2,1,3,0:T(8,128)S(1)} %copy.218, f32[4,32,64,128]{3,2,1,0:T(8,128)} %get-tuple-element.191), kind=kOutput, calls=%fused_computation.75 | convolution fusion | flops 3225387008 | bytes 21626880 | tf_op jit(solution)/shard_map/transpose(jvp(cshp,csn->chpn))/dot_general | solution.py:53
  367.4 37.1 %bitcast_add_fusion.2 = f32[4,256,32,64]{1,3,2,0:T(8,128)} fusion(f32[4,256,32,64]{1,3,2,0:T(8,128)S(1)} %get-tuple-element.333, f32[4,256,32,64]{1,0,3,2:T(4,128)} %reshape.282, f32[4,32,256]{2,1,0:T(8,128)S(1)} %bitcast.275, f32[4,32,256]{2,1,0:T(8,128)S(1)} %copy_bitcast_fusion, f32[4,256,256]{2,1,0:T(8,128)S(1)} %copy-done.25, ...), kind=kOutput, calls=%fused_computation.61 | convolution fusion | flops 6492782592 | bytes 26869888 | tf_op jit(solution)/shard_map/transpose(jvp(chts,cshp->cthp))/dot_general | solution.py:45
  404.6 13.8 %copy.216 = f32[4,256,32,64]{1,0,3,2:T(4,128)} copy(f32[4,256,32,64]{1,3,2,0:T(8,128)} %bitcast_add_fusion.2) | data formatting | bytes 16777216 | tf_op jit(solution)/shard_map/transpose(jvp(chts,cshp->cthp))/add_any | solution.py:45
  427.2 18.0 %fusion.82 = f32[4,256,128]{2,1,0:T(8,128)S(1)} fusion(f32[4,32,64,128]{3,2,1,0:T(8,128)} %get-tuple-element.191, f32[4,256,32,64]{1,0,3,2:T(4,128)} %reshape.275, f32[4,256,32]{1,2,0:T(8,128)S(1)} %get-tuple-element.321), kind=kOutput, calls=%fused_computation.128 | convolution fusion | flops 3223322624 | bytes 13238272 | tf_op jit(solution)/shard_map/transpose(jvp(cshp,csn->chpn))/dot_general | solution.py:53
  445.3 58.1 %fusion.11 = (f32[4,32,256]{2,1,0:T(8,128)}, f32[4,32,256]{2,1,0:T(8,128)}, f32[4,32,256]{2,1,0:T(8,128)S(1)}, f32[4,256,256]{2,1,0:T(8,128)S(1)}) fusion(f32[4,32,256]{2,1,0:T(8,128)S(1)} %bitcast.276, f32[4,32,256]{2,1,0:T(8,128)S(1)} %copy_bitcast_fusion, f32[4,256,256]{2,1,0:T(8,128)S(1)} %copy-done.26, pred[4,256,256]{2,1,0:T(8,128)(4,1)S(1)} %copy-done.28, ...), kind=kOutput, calls=%fused_computation.22 | convolution fusion | flops 6567919616 | bytes 19791872 | tf_op jit(solution)/shard_map/transpose(jvp(chts,cshp->cthp))/dot_general | solution.py:45
  505.6 17.9 %fusion.85 = f32[4,256,128]{2,1,0:T(8,128)S(1)} fusion(f32[4,32,64,128]{3,2,1,0:T(8,128)} %get-tuple-element.482, f32[4,256,32,64]{1,0,3,2:T(4,128)} %reshape.282, f32[4,256,32]{1,2,0:T(8,128)S(1)} %copy-done.23), kind=kOutput, calls=%fused_computation.129 | convolution fusion | flops 3223322624 | bytes 13238272 | tf_op jit(solution)/shard_map/transpose(jvp(ctn,chpn->cthp))/dot_general | solution.py:66
  534.1 10.4 %reduce-window.16 = f32[4,32,2,128]{3,1,2,0:T(8,128)S(1)} reduce-window(f32[4,32,2,128]{3,1,2,0:T(8,128)S(1)} %copy_bitcast_fusion.1, f32[]{:T(128)} %constant.124.clone.1), window={size=1x1x1x128 pad=0_0x0_0x0_0x0_127}, to_apply=%region_16.17 | reduce-window | flops 4161536 | bytes 262148 | tf_op jit(solution)/shard_map/reduce-window.2
  546.2 26.8 %fusion.126 = (f32[2304]{0:T(1024)S(1)}, f32[2304]{0:T(1024)S(1)}, f32[2304]{0:T(1024)S(1)}, f32[2304]{0:T(1024)S(1)}, f32[2304]{0:T(1024)S(1)}, /*index=5*/f32[1024,2304]{0,1:T(8,128)}) fusion(f32[1024,4384]{0,1:T(8,128)} %fusion.91, f32[1024]{0:T(1024)S(1)} %copy-done.50, f32[1024,2304]{0,1:T(8,128)} %copy-done.1, f32[1024]{0:T(1024)S(1)} %copy-done.48, ...), kind=kLoop, calls=%fused_computation.216 | loop fusion | flops 54252288 | bytes 47244288 | tf_op jit(solution)/shard_map/transpose(jvp())/reduce_sum | solution.py:83
  573.0 10.9 %multiply_multiply_fusion.2 = (f32[1024,2304]{0,1:T(8,128)S(1)}, f32[1024,2304]{0,1:T(8,128)S(1)}, f32[1024,2304]{0,1:T(8,128)}, f32[1024,2304]{0,1:T(8,128)}) fusion(f32[1024,2304]{0,1:T(8,128)} %get-tuple-element.298, f32[2304]{0:T(1024)S(1)} %copy-done.38, f32[1024]{0:T(1024)S(1)} %copy-done.52, f32[2304]{0:T(1024)S(1)} %copy-done.36, ...), kind=kLoop, calls=%fused_computation.55 | loop fusion | flops 16515072 | bytes 47235072 | tf_op jit(solution)/shard_map/transpose(jvp())/mul | solution.py:89
  583.9 14.9 %pad_add_fusion = f32[1024,2304]{0,1:T(8,128)} fusion(f32[1024,2304]{0,1:T(8,128)S(1)} %get-tuple-element.313, f32[1024,2304]{0,1:T(8,128)} %get-tuple-element.314, f32[1024,2304]{0,1:T(8,128)} %get-tuple-element.315, f32[1024,2304]{0,1:T(8,128)S(1)} %get-tuple-element.312), kind=kLoop, calls=%fused_computation.46 | loop fusion | flops 7077888 | bytes 47185920 | tf_op jit(solution)/shard_map/transpose(jvp())/add_any | solution.py:85
  598.8 21.9 %fusion.89 = f32[1024,4384]{0,1:T(8,128)} fusion(bf16[1,1024,1024]{2,1,0:T(8,128)(2,1)S(1)} %copy-done.7, f32[1024]{0:T(1024)S(1)} %copy-done.66, f32[1024]{0:T(1024)S(1)} %copy-done.68, f32[1024,2048]{0,1:T(8,128)} %get-tuple-element.311, f32[1024,2304]{0,1:T(8,128)} %pad_add_fusion, f32[1024,32]{0,1:T(8,128)S(1)} %get-tuple-element.297), kind=kOutput, calls=%fused_computation.132 | convolution fusion | flops 9211576320 | bytes 38019072 | tf_op jit(solution)/shard_map/dot_general | solution.py:129
  623.0 161.2 %reduce-scatter.6.cloned.1.call-done = f32[256,4384]{0,1:T(8,128)} async-done(((f32[1024,4384]{0,1:T(8,128)}), f32[256,4384]{0,1:T(8,128)}) %reduce-scatter.6.cloned.1.call-update) | async-done | bytes 4489232 | tf_op jit(solution)/shard_map/reduce_scatter | solution.py:191
  784.3 18.4 %fusion.65 = (f32[1024]{0:T(1024)S(1)}, f32[1024]{0:T(1024)S(1)}, f32[1024,1024]{1,0:T(8,128)}) fusion(bf16[1,1024,1024]{2,1,0:T(8,128)(2,1)S(1)} %copy-done.7, f32[1024]{0:T(1024)S(1)} %copy-done.68, f32[1024]{0:T(1024)S(1)} %copy-done.66, bf16[1024,4384]{0,1:T(8,128)(2,1)} %all-gather.4.cloned.1.call-done, f32[1024,2048]{0,1:T(8,128)} %get-tuple-element.311, ...), kind=kOutput, calls=%fused_computation.106 | convolution fusion | flops 9214720000 | bytes 33243136 | tf_op jit(solution)/shard_map/dot_general | solution.py:135
  803.7 12.1 %all-reduce.24 = f32[5472]{0:T(1024)S(1)} all-reduce(f32[5472]{0:T(1024)S(1)} %pad_add_fusion.4), channel_id=5, replica_groups=mesh['grp'=4,'dp'=8] {'grp'}, use_global_device_ids=true, to_apply=%region_37.38.clone | all-reduce | flops 5472 | bytes 43776
  821.0 9.5 fusion.77
  831.5 27.6 %all-reduce.25 = (f32[4,576]{1,0:T(4,128)S(1)}, f32[1368]{0:T(1024)S(1)}) all-reduce(f32[4,576]{1,0:T(4,128)S(1)} %copy.237, f32[1368]{0:T(1024)S(1)} %dynamic-slice.2), channel_id=1, replica_groups=mesh['grp'=4,'dp'=8] {'dp'}, use_global_device_ids=true, to_apply=%region_29.30 | all-reduce | flops 3672 | bytes 29376 | tf_op jit(solution)/shard_map/psum | solution.py:196
  860.4 101.6 %all-reduce.29.cloned.1.call-done = (f32[256,4384]{0,1:T(8,128)}, f32[512,1024]{1,0:T(8,128)}) async-done(((f32[256,4384]{0,1:T(8,128)}, f32[512,1024]{1,0:T(8,128)}), (f32[256,4384]{0,1:T(8,128)}, f32[512,1024]{1,0:T(8,128)})) %all-reduce.29.cloned.1.call-update) | async-done | bytes 6586384 | tf_op jit(solution)/shard_map/psum | solution.py:196
  962.0 12.3 %multiply_subtract_fusion = (f32[256,4384]{0,1:T(8,128)}, f32[256,4384]{0,1:T(8,128)}, f32[256,4384]{0,1:T(8,128)}) fusion(f32[256,4384]{0,1:T(8,128)} %param.22, f32[256,4384]{0,1:T(8,128)} %get-tuple-element.286, f32[256,4384]{0,1:T(8,128)} %param.26, f32[256,4384]{0,1:T(8,128)} %param.30), kind=kLoop, calls=%fused_computation.104 | loop fusion | flops 15712256 | bytes 31424512 | tf_op jit(solution)/shard_map/sub | solution.py:121
  (326 shorter events, 142.0 us)
Async XLA Ops:
  7.2 98.9 %all-gather.4.cloned.1.call-start = ((), (), s32[]{:S(2)}) async-start(), calls=%async_computation.3 | async-start | bytes 11223040 | tf_op jit(solution)/shard_map/all_gather | solution.py:158
  11.3 276.6 %all-gather.6.cloned.1.call-start = ((), (), s32[]{:S(2)}) async-start(), calls=%async_computation.4 | async-start | bytes 5242880 | tf_op jit(solution)/shard_map/all_gather | solution.py:159
  14.1 608.9 %reduce-scatter.8.cloned.1.call-start = ((), (), s32[]{:S(2)}) async-start(), calls=%async_computation.6 | async-start | bytes 10485760 | tf_op jit(solution)/shard_map/reduce_scatter | solution.py:192
  29.1 92.8 %copy-start.65 = (f32[1024]{0:T(1024)}, f32[1024]{0:T(1024)S(1)}, u32[]{:S(2)}) copy-start(f32[1024]{0:T(1024)S(1)} %slice.123) | copy-start | bytes 12292
  29.1 92.8 %copy-start.64 = (f32[5472]{0:T(1024)}, f32[5472]{0:T(1024)S(1)}, u32[]{:S(2)}) copy-start(f32[5472]{0:T(1024)S(1)} %convert_element_type.67) | copy-start | bytes 65668
  29.7 118.7 %copy-start.79 = (f32[32]{0:T(128)}, f32[32]{0:T(128)S(1)}, u32[]{:S(2)}) copy-start(f32[32]{0:T(128)S(1)} %get-tuple-element.323) | copy-start | bytes 388
  38.2 88.3 %copy-start.35 = (f32[2304]{0:T(1024)}, f32[2304]{0:T(1024)S(1)}, u32[]{:S(2)}) copy-start(f32[2304]{0:T(1024)S(1)} %get-tuple-element.254) | copy-start | bytes 27652
  38.2 88.3 %copy-start.37 = (f32[2304]{0:T(1024)}, f32[2304]{0:T(1024)S(1)}, u32[]{:S(2)}) copy-start(f32[2304]{0:T(1024)S(1)} %get-tuple-element.255) | copy-start | bytes 27652
  38.2 88.3 %copy-start.39 = (f32[2304]{0:T(1024)}, f32[2304]{0:T(1024)S(1)}, u32[]{:S(2)}) copy-start(f32[2304]{0:T(1024)S(1)} %get-tuple-element.256) | copy-start | bytes 27652
  38.2 88.3 %copy-start.41 = (f32[2304]{0:T(1024)}, f32[2304]{0:T(1024)S(1)}, u32[]{:S(2)}) copy-start(f32[2304]{0:T(1024)S(1)} %get-tuple-element.257) | copy-start | bytes 27652
  38.3 88.3 %copy-start.47 = (f32[1024]{0:T(1024)}, f32[1024]{0:T(1024)S(1)}, u32[]{:S(2)}) copy-start(f32[1024]{0:T(1024)S(1)} %get-tuple-element.326) | copy-start | bytes 12292
  38.3 88.3 %copy-start.49 = (f32[1024]{0:T(1024)}, f32[1024]{0:T(1024)S(1)}, u32[]{:S(2)}) copy-start(f32[1024]{0:T(1024)S(1)} %get-tuple-element.327) | copy-start | bytes 12292
  38.3 88.3 %copy-start.51 = (f32[1024]{0:T(1024)}, f32[1024]{0:T(1024)S(1)}, u32[]{:S(2)}) copy-start(f32[1024]{0:T(1024)S(1)} %get-tuple-element.328) | copy-start | bytes 12292
  38.8 83.0 %copy-start.57 = (f32[1024]{0:T(1024)}, f32[1024]{0:T(1024)S(1)}, u32[]{:S(2)}) copy-start(f32[1024]{0:T(1024)S(1)} %fusion.68) | copy-start | bytes 12292
  38.9 83.0 %copy-start.67 = (f32[1024]{0:T(1024)}, f32[1024]{0:T(1024)S(1)}, u32[]{:S(2)}) copy-start(f32[1024]{0:T(1024)S(1)} %fusion.119) | copy-start | bytes 12292
  38.9 110.5 %copy-start.83 = (f32[32]{0:T(128)}, f32[32]{0:T(128)S(1)}, u32[]{:S(2)}) copy-start(f32[32]{0:T(128)S(1)} %fusion.122) | copy-start | bytes 388
  40.2 123.4 %copy-start.81 = (f32[4]{0:T(128)}, f32[4]{0:T(128)S(1)}, u32[]{:S(2)}) copy-start(f32[4]{0:T(128)S(1)} %fusion.121) | copy-start | bytes 52
  40.3 123.3 %copy-start.43 = (f32[4,256]{1,0:T(4,128)}, f32[4,256]{1,0:T(4,128)S(1)}, u32[]{:S(2)}) copy-start(f32[4,256]{1,0:T(4,128)S(1)} %get-tuple-element.325) | copy-start | bytes 12292
  40.3 123.3 %copy-start.55 = (f32[4,256]{1,0:T(4,128)}, f32[4,256]{1,0:T(4,128)S(1)}, u32[]{:S(2)}) copy-start(f32[4,256]{1,0:T(4,128)S(1)} %get-tuple-element.324) | copy-start | bytes 12292
  149.5 39.9 %copy-start.9 = (f32[1024,32]{0,1:T(8,128)}, f32[1024,32]{0,1:T(8,128)S(1)}, u32[]{:S(2)}) copy-start(f32[1024,32]{0,1:T(8,128)S(1)} %compare_select_fusion.2) | copy-start | bytes 393220
  163.8 162.5 %copy-start.22 = (f32[4,256,32]{1,2,0:T(8,128)}, f32[4,256,32]{1,2,0:T(8,128)S(1)}, u32[]{:S(2)}) copy-start(f32[4,256,32]{1,2,0:T(8,128)S(1)} %get-tuple-element.320) | copy-start | bytes 393220
  190.7 59.1 %copy-start.15 = (f32[4,256,128]{2,1,0:T(8,128)}, f32[4,256,128]{2,1,0:T(8,128)S(1)}, u32[]{:S(2)}) copy-start(f32[4,256,128]{2,1,0:T(8,128)S(1)} %copy.181) | copy-start | bytes 1572868
  427.2 357.1 %reduce-scatter.6.cloned.1.call-start = ((), (), s32[]{:S(2)}) async-start(), calls=%async_computation.5 | async-start | bytes 22446080 | tf_op jit(solution)/shard_map/reduce_scatter | solution.py:191
  445.3 58.1 %copy-start.16 = (f32[4,256,128]{2,1,0:T(8,128)S(1)}, f32[4,256,128]{2,1,0:T(8,128)}, u32[]{:S(2)}) copy-start(f32[4,256,128]{2,1,0:T(8,128)} %copy-done.15) | copy-start | bytes 1572868
  445.3 60.2 %copy-start.23 = (f32[4,256,32]{1,2,0:T(8,128)S(1)}, f32[4,256,32]{1,2,0:T(8,128)}, u32[]{:S(2)}) copy-start(f32[4,256,32]{1,2,0:T(8,128)} %copy-done.22) | copy-start | bytes 393220
  620.7 209.7 %reduce-scatter.10.cloned.1.call-start = ((), (), s32[]{:S(2)}) async-start(), calls=%async_computation.7 | async-start | bytes 1474560
  622.3 339.7 %all-reduce.29.cloned.1.call-start = ((), (), s32[]{:S(2)}) async-start(), calls=%async_computation.8 | async-start | bytes 13172736 | tf_op jit(solution)/shard_map/psum | solution.py:196
  820.9 38.2 %copy-start.63 = (f32[1368]{0:T(1024)S(1)}, f32[1368]{0:T(1024)}, u32[]{:S(2)}) copy-start(f32[1368]{0:T(1024)} %param.25) | copy-start | bytes 16420
  820.9 38.2 %copy-start.74 = (f32[1368]{0:T(1024)S(1)}, f32[1368]{0:T(1024)}, u32[]{:S(2)}) copy-start(f32[1368]{0:T(1024)} %param.29) | copy-start | bytes 16420
  820.9 38.8 %copy-start.54 = (f32[4,576]{1,0:T(4,128)S(1)}, f32[4,576]{1,0:T(4,128)}, u32[]{:S(2)}) copy-start(f32[4,576]{1,0:T(4,128)} %param.24) | copy-start | bytes 27652
  821.0 38.8 %copy-start.72 = (f32[4,576]{1,0:T(4,128)S(1)}, f32[4,576]{1,0:T(4,128)}, u32[]{:S(2)}) copy-start(f32[4,576]{1,0:T(4,128)} %param.28) | copy-start | bytes 27652
  821.0 38.8 %copy-start.73 = (f32[4,576]{1,0:T(4,128)S(1)}, f32[4,576]{1,0:T(4,128)}, u32[]{:S(2)}) copy-start(f32[4,576]{1,0:T(4,128)} %param.32) | copy-start | bytes 27652
  (63 other events, 1038.9 us)
Sparse Core Ops, SparseCore 0:
  11.4 94.6 all-gather.3
  108.6 52.6 all-gather.5
  427.3 86.3 reduce-scatter.7
  620.9 163.3 reduce-scatter.5
  787.6 29.1 reduce-scatter.9
  819.2 142.7 all-reduce.28
where the time goes:
time: 1000 us; the launch traced here: 986 us
  waiting for transfers between devices  329 us (33%)
  matrix products  314 us (31%)
  other arithmetic  168 us (17%)
  local copies, waits for them, and re-layouts  99.4 us (10%)
  blocking collectives  59.3 us (6%)
  between operations  17 us (2%)
    reduce_scatter x1, waiting for transfers between devices, local(): lax.psum_scatter(grad_in, 'grp', scatter_dimension=0, tiled=True)  161 us
    dot_general x3, matrix products, state_scan(): jnp.einsum('chts,cshp->cthp', weights, x_blocks, precision=highest)  140 us
    psum x1, waiting for transfers between devices, local(): lax.psum((in_share, out_share, filter_share, vector_share), 'dp')  102 us
    all_gather x1, waiting for transfers between devices, local(): lax.all_gather(in_weight.astype(jnp.bfloat16), 'grp', axis=0, tiled=True)  65.8 us
    dot_general x3, matrix products, state_scan(): jnp.einsum('cshp,csn->chpn', weighted_x, b_blocks, precision=highest)  44.6 us
    dot_general x3, matrix products, state_scan(): jnp.einsum('ctn,chpn->cthp', c_blocks, entering, precision=highest)  40.3 us
    dot_general x2, matrix products, contract_cols(): lax.dot_general(left, right, (((1,), (1,)), ((), ())), preferred_element_...  30 us
    dot_general x2, matrix products, contract_rows(): lax.dot_general(left, right, (((0,), (0,)), ((), ())), preferred_element_...  29.2 us
  transfers between devices with their start and end apart: 6, of which 3 were waited for; matrix products, arithmetic and copies ran while one was open for 42% of the time, Pallas kernels for 0%

commit v1 on v0

v1 whole, which is shorter than its diff:
```python
import functools
import math

import jax
import jax.numpy as jnp
from jax import lax
from jax.experimental import pallas as pl
from jax.experimental.pallas import tpu as pltpu
from jax.sharding import PartitionSpec as P

D = 1024
H = 32
P_SIZE = 64
NSTATE = 128
KERNEL = 4
STEP = 7
D_INNER = 2048
CONV_CH = 2304
XBC = D_INNER + CONV_CH
LANES = 128
T = 256
W = 256
HPT = W // P_SIZE
NT = D_INNER // W
CT = CONV_CH // W
SMALL_COLS = 1408
CHUNK = 32
HEADS_AT = D + D_INNER + CONV_CH
VEC = HEADS_AT + 3 * H
VEC_PAD = 5504
STEP_AT = D_INNER + CONV_CH
ALL = STEP_AT + LANES
LOG2E = math.log2(math.e)

EPSILON = 1e-05
ADAM_EPSILON = 1e-08
BETA_FIRST = 0.5
BETA_SECOND = 0.5
WEIGHT_DECAY = 0.1

F32 = jnp.float32
BF16 = jnp.bfloat16
HIGHEST = lax.Precision.HIGHEST
VMEM_LIMIT = 58 * 1024 * 1024


def dot_nn(a, b):
    return lax.dot_general(a, b, (((1,), (0,)), ((), ())), preferred_element_type=F32)


def dot_nt(a, b):
    return lax.dot_general(a, b, (((1,), (1,)), ((), ())), preferred_element_type=F32)


def dot_tn(a, b):
    return lax.dot_general(a, b, (((0,), (0,)), ((), ())), preferred_element_type=F32)


def sigmoid(v):
    return 0.5 * jnp.tanh(0.5 * v) + 0.5


def rows8(v):
    return jnp.sum(v.reshape(v.shape[0] // 8, 8, v.shape[1]), axis=0)


def tile_of(i):
    return slice(i * W, (i + 1) * W)


def tile_at(i, width=W):
    return pl.ds(pl.multiple_of(i * width, width), width)


def whole(shape):
    zeros = (0,) * len(shape)
    return pl.BlockSpec(shape, lambda *_: zeros, pipeline_mode=pl.Buffered(1))


MESH = pl.DeviceIdType.MESH
HOPS = (("dp", 1), ("grp", 1), ("grp", 2), ("dp", 2), ("dp", 4))
CORE, ALONG_X, ALONG_Y, Z_NEAR, Z_FAR = range(5)


def bit(hop):
    name, size = HOPS[hop]
    return lax.rem(lax.div(lax.axis_index(name), size), 2)


def across(hop):
    name, size = HOPS[hop]
    return {name: lax.axis_index(name) + size * (1 - 2 * bit(hop))}


def greet(hops):
    barrier = pltpu.get_barrier_semaphore()
    for hop in hops:
        pl.semaphore_signal(barrier, inc=1, device_id=across(hop), device_id_type=MESH)
    pl.semaphore_wait(barrier, len(hops))


def rows_at(start, size):
    return pl.ds(pl.multiple_of(start, size), size)


def add_rows(out, a, b):
    out[...] = a[...] + b[...]


def reduce_chunk(src, cols, first_x, bufs, total, sends, recvs, index, local_sem):
    own, r1, r2, r3, r4, r0 = bufs
    rows = src.shape[2]
    half, quarter, eighth = rows // 2, rows // 4, rows // 8
    c, x, y, z1, z2 = (bit(hop) for hop in range(5))
    first, second = (ALONG_X, ALONG_Y) if first_x else (ALONG_Y, ALONG_X)
    base = c * half
    base1 = base + z1 * quarter
    base2 = base1 + z2 * eighth

    def copy(n, hop, a, b):
        return pltpu.make_async_remote_copy(
            src_ref=a, dst_ref=b, send_sem=sends.at[index, n], recv_sem=recvs.at[index, n],
            device_id=across(hop), device_id_type=MESH,
        )

    def pair(u):
        return own.at[:, u] if first_x else own.at[u]

    kept = bit(first)
    load = pltpu.make_async_copy(src.at[:, :, rows_at(base, half), cols], own, local_sem)
    here = [total.at[rows_at(base2, eighth)], total.at[rows_at(base1, quarter)], total.at[rows_at(base, half)]]
    copies = [
        copy(0, CORE, src.at[:, :, rows_at((1 - c) * half, half), cols], r0),
        copy(1, first, pair(1 - kept), r1),
        copy(2, second, r1.at[1 - bit(second)], r2),
        copy(3, Z_NEAR, r2.at[rows_at((1 - z1) * quarter, quarter)], r3),
        copy(4, Z_FAR, r3.at[rows_at((1 - z2) * eighth, eighth)], r4),
        copy(5, Z_FAR, here[0], here[0]),
        copy(6, Z_NEAR, here[1], here[1]),
        copy(7, CORE, here[2], here[2]),
    ]

    def begin():
        load.start()
        copies[0].start()

    def after_core():
        load.wait()
        copies[0].wait_recv()
        add_rows(own, own, r0)
        copies[1].start()

    def after_first():
        copies[1].wait_recv()
        add_rows(r1, r1, pair(kept))
        copies[2].start()

    def after_second():
        copies[2].wait_recv()
        add_rows(r2, r2, r1.at[bit(second)])
        copies[3].start()

    def after_near():
        copies[3].wait_recv()
        add_rows(r3, r3, r2.at[rows_at(z1 * quarter, quarter)])
        copies[4].start()

    def after_far():
        copies[4].wait_recv()
        add_rows(here[0], r4, r3.at[rows_at(z2 * eighth, eighth)])
        copies[5].start()

    def gather_far():
        copies[5].wait_recv()
        copies[6].start()

    def gather_near():
        copies[6].wait_recv()
        copies[7].start()

    def arrive():
        copies[7].wait_recv()

    def finish():
        for one in copies:
            one.wait_send()

    return (begin, after_core, after_first, after_second, after_near, after_far, gather_far, gather_near, arrive), finish


def reduce_buffers(rows, cols, count, dtype=BF16):
    half = rows // 2
    shapes = [
        (2, 2, half, cols), (2, 2, half, cols), (2, half, cols), (half, cols), (half // 2, cols), (half // 4, cols), (rows, cols),
    ]
    return [pltpu.VMEM((count, *shape), dtype) for shape in shapes]


BUFFERS = 7
STAGES = 9


def reduce_plan(src, starts, size, slots, pace, bufs, result, sems, base, x_first):
    local_sems, out_sems, sends, recvs = sems
    ticks, ends = [], []
    for n, (start, slot) in enumerate(zip(starts, slots)):
        index = base + n
        own, r0, r1, r2, r3, r4, total = (ref.at[n] for ref in bufs)
        cols = pl.ds(start, size)
        stages, finish = reduce_chunk(
            src, cols, x_first[n], (own, r1, r2, r3, r4, r0), total, sends, recvs, index, local_sems.at[index]
        )
        write = pltpu.make_async_copy(total, result.at[:, cols], out_sems.at[index])
        for later, stage in zip(pace, stages):
            ticks.append((slot + later, stage))
        ticks.append((slot + pace[-1], write.start))
        ends += [finish, write.wait]
    return ticks, ends


def small_plan(src, bufs, total, sems, slot, spacing):
    sends, recvs = sems
    r0, a1, r1, a2, r2, a3, r3, a4, r4 = bufs
    x, y = bit(ALONG_X), bit(ALONG_Y)

    def copy(n, hop, a, b):
        return pltpu.make_async_remote_copy(
            src_ref=a, dst_ref=b, send_sem=sends.at[n], recv_sem=recvs.at[n], device_id=across(hop), device_id_type=MESH
        )

    copies = [
        copy(0, CORE, src, r0),
        copy(1, ALONG_X, a1.at[:, 1 - x], r1),
        copy(2, ALONG_Y, a2.at[1 - y], r2),
        copy(3, Z_NEAR, a3, r3),
        copy(4, Z_FAR, a4, r4),
    ]

    def after(n, out, one, other):
        def stage():
            copies[n].wait_recv()
            out[...] = one[...] + other[...]
            if n < 4:
                copies[n + 1].start()

        return stage

    stages = [
        copies[0].start,
        after(0, a1, src, r0),
        after(1, a2, a1.at[:, x], r1),
        after(2, a3, a2.at[y], r2),
        after(3, a4, a3, r3),
        after(4, total, a4, r4),
    ]
    return [(slot + k * spacing, stage) for k, stage in enumerate(stages)], [one.wait_send for one in copies]


def small_buffers(rows, cols):
    shapes = [(2, 2, rows, cols), (2, 2, rows, cols), (2, rows, cols), (2, rows, cols)] + [(rows, cols)] * 5
    return [pltpu.VMEM(shape, F32) for shape in shapes]


def by_slot(ticks):
    slots = {}
    for slot, action in ticks:
        slots.setdefault(slot, []).append(action)
    return slots


def head_terms(sraw_ref, hv_ref):
    v = sraw_ref[...] + hv_ref[0:1, :]
    step = jnp.maximum(v, 0.0) + jnp.log1p(jnp.exp(-jnp.abs(v)))
    rate = -jnp.exp(hv_ref[1:2, :])
    return v, step, rate


def before(rows, cols):
    return lax.broadcasted_iota(jnp.int32, (rows, cols), 0), lax.broadcasted_iota(jnp.int32, (rows, cols), 1)


def cumulate(logdecay):
    t, s = before(T, T)
    lower = jnp.where(s <= t, 1.0, 0.0)
    return jnp.dot(lower, logdecay * LOG2E, precision=HIGHEST, preferred_element_type=F32)


def spread(cum, cum_b):
    for h in range(H):
        cum_b[h] = jnp.broadcast_to(cum[:, h : h + 1], (T, LANES))


def expand(values, fan, out):
    high = values.astype(BF16)
    low = (values - high.astype(F32)).astype(BF16)
    both = jnp.concatenate([high, low], axis=1)
    for c in range(0, D_INNER, 2 * W):
        out[:, c : c + 2 * W] = dot_nn(both, fan[:, c : c + 2 * W])


def set_fan(fan):
    for c in range(0, D_INNER, W):
        row, lane = before(2 * LANES, W)
        fan[:, c : c + W] = jnp.where(lax.shift_right_logical(lane + c, 6) == (row & (LANES - 1)), 1.0, 0.0).astype(BF16)


def put_diagonal(diag, r, tile):
    lane = lax.broadcasted_iota(jnp.int32, (tile.shape[0], LANES), 1)
    first = jnp.where(lane < P_SIZE, 1.0, 0.0).astype(BF16)
    second = jnp.where(lane < P_SIZE, 0.0, 1.0).astype(BF16)
    for k in range(HPT):
        at = LANES * (k // 2)
        part = tile[:, at : at + LANES]
        diag[k * T + r : k * T + r + tile.shape[0], at : at + LANES] = part * (first if k % 2 == 0 else second)


def from_start_last(cum_b, i):
    lane = lax.broadcasted_iota(jnp.int32, (1, LANES), 1)
    last = slice(T - 1, T)
    halves = [jnp.where(lane < P_SIZE, cum_b[HPT * i + 2 * k, last], cum_b[HPT * i + 2 * k + 1, last]) for k in range(2)]
    return jnp.exp2(jnp.concatenate(halves, axis=1))


def wide(m):
    return jnp.concatenate([m, m], axis=1)


def split_halves(values, high_ref, low_ref, rows):
    high = values.astype(BF16)
    high_ref[rows] = high
    low_ref[rows] = (values - high.astype(F32)).astype(BF16)


def head_sums(high_ref, low_ref, pick):
    return dot_nn(high_ref[...], pick) + dot_nn(low_ref[...], pick)


def set_pick(pick):
    for r in range(0, D_INNER, T):
        row, lane = before(T, LANES)
        pick[r : r + T] = jnp.where(lax.shift_right_logical(row + r, 6) == lane, 1.0, 0.0).astype(BF16)


def chunks(start=0, stop=T):
    return [slice(r, r + CHUNK) for r in range(start, stop, CHUNK)]


def scan_forward(block, act, sraw_ref, segb_ref, seg_ref, hv_ref, skip_ref, y_ref, st_ref, scratch):
    (
        state, cum_b, fan, wcat, cum_rows, xw_scr, carr_scr, diag, scores, prev_seg, step_f, from_start, to_end,
    ) = scratch
    tokens = rows_at(block * T, T)

    @pl.when(block == 0)
    def _():
        state[...] = jnp.zeros_like(state)
        wcat[...] = jnp.zeros_like(wcat)
        diag[...] = jnp.zeros_like(diag)
        prev_seg[...] = jnp.full(prev_seg.shape, -1.0, F32)
        set_fan(fan)

    _, step, rate = head_terms(sraw_ref.at[tokens], hv_ref)
    cum = cumulate(step * rate)
    cum_rows[...] = cum.T
    spread(cum, cum_b)
    bmat = act[tokens, D_INNER : D_INNER + NSTATE]
    cmat = act[tokens, D_INNER + NSTATE : CONV_CH]
    segb = segb_ref[tokens]
    t_at, s_at = before(T, T)
    valid = (wide(segb) == seg_ref[0:1, tokens].astype(F32)) & (s_at <= t_at)
    scores[...] = jnp.where(valid, dot_nt(cmat, bmat), 0.0).astype(BF16)
    prev = prev_seg[0:1]
    last_seg = segb[T - 1 : T]
    last = cum[T - 1 : T]
    expand(step, fan, step_f)
    expand(jnp.exp2(cum) * jnp.where(segb == prev, 1.0, 0.0), fan, from_start)
    expand(jnp.exp2(last - cum) * jnp.where(segb == last_seg, 1.0, 0.0), fan, to_end)
    keep = wide(jnp.where(last_seg == prev, 1.0, 0.0))
    prev_seg[0:1] = last_seg
    b_t = bmat.astype(F32).T.astype(BF16)
    st_ref[0] = state[...].astype(BF16)
    carr_scr[...] = dot_nn(cmat, st_ref[0])

    def group(i, _):
        cols = tile_at(i)
        for rows in chunks():
            here = pl.ds(pl.multiple_of(block * T + rows.start, CHUNK), CHUNK)
            x1 = (act[here, cols].astype(F32) * step_f[rows, cols]).astype(BF16)
            put_diagonal(diag, rows.start, x1)
            xw_scr[rows, cols] = (x1.astype(F32) * to_end[rows, cols]).astype(BF16)
        for k in range(HPT):
            row = cum_rows[pl.ds(HPT * i + k, 1), :]
            for rows in chunks():
                n = LANES if rows.start < LANES else T
                colb = cum_b[HPT * i + k, rows]
                colb = colb if n == LANES else wide(colb)
                decay = jnp.exp2(jnp.minimum(colb - row[:, :n], 0.0)).astype(BF16)
                wcat[rows, k * T : k * T + n] = scores[rows, :n] * decay
        y_ref[:, cols] = dot_nn(wcat[...], diag[...])
        skip = skip_ref[0:1, cols]
        for rows in chunks():
            here = pl.ds(pl.multiple_of(block * T + rows.start, CHUNK), CHUNK)
            y = y_ref[rows, cols] + carr_scr[rows, cols] * from_start[rows, cols]
            y_ref[rows, cols] = y + act[here, cols].astype(F32) * skip
        fade = from_start_last(cum_b, i) * keep
        for rows in chunks(0, NSTATE):
            state[rows, cols] = state[rows, cols] * fade
        return 0

    lax.fori_loop(0, NT, group, 0)
    state[...] += dot_nn(b_t, xw_scr[...])


def scan_scratch():
    return [
        pltpu.VMEM((NSTATE, D_INNER), F32),
        pltpu.VMEM((H, T, LANES), F32),
        pltpu.VMEM((2 * LANES, D_INNER), BF16),
        pltpu.VMEM((T, HPT * T), BF16),
        pltpu.VMEM((LANES, T), F32),
        pltpu.VMEM((T, D_INNER), BF16),
        pltpu.VMEM((T, D_INNER), F32),
        pltpu.VMEM((HPT * T, W), BF16),
        pltpu.VMEM((T, T), BF16),
        pltpu.VMEM((8, LANES), F32),
        pltpu.VMEM((T, D_INNER), F32),
        pltpu.VMEM((T, D_INNER), F32),
        pltpu.VMEM((T, D_INNER), F32),
    ]


def norm_rows(tok_ref, gain, nrm_ref):
    def body(i, _):
        rows = pl.ds(pl.multiple_of(i * CHUNK, CHUNK), CHUNK)
        tok = tok_ref[rows].astype(F32)
        rho = lax.rsqrt(jnp.sum(tok * tok, axis=1, keepdims=True) * (1.0 / D) + EPSILON)
        nrm_ref[rows] = (tok * rho * gain).astype(BF16)
        return 0

    lax.fori_loop(0, tok_ref.shape[0] // CHUNK, body, 0)


def segment_masks(seg_ref, segb_ref, pad, mask):
    length = segb_ref.shape[0]
    column = jnp.broadcast_to(seg_ref[...].astype(F32), (8, length)).T
    pad[0:8] = jnp.full((8, LANES), -1.0, F32)
    for r in range(0, length, T):
        rows = jnp.broadcast_to(column[r : r + T, 0:1], (T, LANES))
        segb_ref[r : r + T] = rows
        pad[8 + r : 8 + r + T] = rows
    for k in range(1, KERNEL):
        for r in range(0, length, T):
            mask[k - 1, r : r + T] = jnp.where(pad[8 + r - k : 8 + r - k + T] == segb_ref[r : r + T], 1.0, 0.0)


def unpack_small(slots, taps_ref, vec_ref, hv_ref, skip_ref):
    parts = slots.shape[0]
    taps_ref[...] = jnp.zeros_like(taps_ref)
    vec_ref[...] = jnp.zeros_like(vec_ref)
    hv_ref[...] = jnp.zeros_like(hv_ref)
    skip_ref[...] = jnp.zeros_like(skip_ref)
    n, m = CONV_CH // parts, VEC // parts
    for p in range(parts):
        taps_ref[0:KERNEL, n * p : n * (p + 1)] = slots[p, 0:KERNEL, 0:n].astype(BF16).astype(F32)
        vec_ref[0:1, m * p : m * (p + 1)] = slots[p, 8:9, 0:m].astype(BF16).astype(F32)
    for k in range(2):
        hv_ref[k : k + 1, 0:H] = vec_ref[0:1, HEADS_AT + k * H : HEADS_AT + (k + 1) * H]
    for h in range(H):
        at = HEADS_AT + 2 * H + h
        skip_ref[0:1, P_SIZE * h : P_SIZE * (h + 1)] = jnp.broadcast_to(vec_ref[0:1, at : at + 1], (1, P_SIZE))


def conv_tile(j, nrm_ref, w, taps_ref, vec_ref, mask, act_ref, dsilu_ref, cin_ref, pad):
    length = nrm_ref.shape[0]
    pad[0:8] = jnp.zeros((8, W), F32)
    cols = tile_at(j)
    taps = [taps_ref[k : k + 1, cols] for k in range(KERNEL)]
    bias = vec_ref[0:1, pl.ds(pl.multiple_of(D + D_INNER + j * W, W), W)]
    for top in range(0, length, T):
        pad[8 + top : 8 + top + T] = dot_nn(nrm_ref[top : top + T], w[:, cols])
        for r in range(top, top + T, CHUNK):
            here = pad[8 + r : 8 + r + CHUNK]
            cin_ref[r : r + CHUNK] = here.astype(BF16)
            total = bias + here * taps[0]
            for k in range(1, KERNEL):
                m = wide(mask[k - 1, r : r + CHUNK])
                total = total + pad[8 + r - k : 8 + r - k + CHUNK] * m * taps[k]
            sig = sigmoid(total)
            act = total * sig
            act_ref[r : r + CHUNK] = act.astype(BF16)
            dsilu_ref[r : r + CHUNK] = (sig + act * (1.0 - sig)).astype(BF16)


def weight_piece(src, src_cols, put, hop_sems, index, rows):
    sends, recvs = hop_sems
    half, quarter = rows // 2, rows // 4
    me = lax.axis_index("grp")
    x, y = bit(ALONG_X), bit(ALONG_Y)
    slot_x, slot_y, slot_d = 2 * y + 1 - x, 2 * (1 - y) + x, 2 * (1 - y) + 1 - x
    top = bit(CORE) * half

    def copy(n, a, b, hop):
        return pltpu.make_async_remote_copy(
            src_ref=a, dst_ref=b, send_sem=sends.at[index, n], recv_sem=recvs.at[index, n],
            device_id=across(hop), device_id_type=MESH,
        )

    def onward(n, slot, start, size, hop):
        return copy(n, put(slot * rows + start, size), put(slot * rows + start, size), hop)

    mine = src.at[rows_at(top, half), src_cols]
    copies = [
        copy(0, mine, put(me * rows + top, half), ALONG_X),
        copy(1, mine, put(me * rows + top, half), ALONG_Y),
        onward(2, slot_x, top, quarter, ALONG_Y),
        onward(3, slot_y, top + quarter, quarter, ALONG_X),
        onward(4, slot_x, top, half, CORE),
        onward(5, slot_y, top, half, CORE),
        onward(6, slot_d, top, quarter, CORE),
        onward(7, slot_d, top + quarter, quarter, CORE),
    ]

    def own():
        copies[0].start()
        copies[1].start()

    def pass_on():
        copies[0].wait_recv()
        copies[2].start()
        copies[1].wait_recv()
        copies[3].start()
        copies[4].start()
        copies[5].start()

    def corner():
        copies[2].wait_recv()
        copies[6].start()
        copies[3].wait_recv()
        copies[7].start()

    def arrive():
        for n in range(4, 8):
            copies[n].wait_recv()

    def finish():
        for one in copies:
            one.wait_send()

    return own, pass_on, corner, arrive, finish


def project_kernel(
    tok_ref, seg_ref, wt_ref, wo_ref, small_ref,
    act_ref, dsilu_ref, cin_ref, y_ref, st_ref, sraw_ref, nrm_ref, segb_ref, taps_ref, vec_ref, hv_ref, skip_ref,
    wg_full, wc_full, wo_full,
    wt_f32, wo_f32, stage_in, stage_out, conv_full, slots, pad, segpad, mask, act, *rest,
):
    *scan, local_sems, sends, recvs, small_sends, small_recvs = rest
    j = pl.program_id(0)
    me = lax.axis_index("grp")
    rows_in, rows_out = D // 4, D_INNER // 4
    load_conv = pltpu.make_async_copy(wt_ref.at[D_INNER:], wt_f32.at[D_INNER : D_INNER + CONV_CH + H], local_sems.at[0])
    load_gate = pltpu.make_async_copy(wt_ref.at[:D_INNER], wt_f32.at[:D_INNER], local_sems.at[1])
    load_out = pltpu.make_async_copy(wo_ref, wo_f32, local_sems.at[2])
    keep_conv = pltpu.make_async_copy(
        stage_in.at[:, D_INNER:], conv_full.at[rows_at(me * rows_in, rows_in)], local_sems.at[3]
    )
    keep_gate = pltpu.make_async_copy(
        stage_in.at[:, :D_INNER], wg_full.at[rows_at(me * rows_in, rows_in)], local_sems.at[4]
    )
    keep_out = pltpu.make_async_copy(stage_out, wo_full.at[rows_at(me * rows_out, rows_out)], local_sems.at[5])
    write_conv = pltpu.make_async_copy(conv_full, wc_full, local_sems.at[6])

    def small_copy(n, a, b, hop):
        return pltpu.make_async_remote_copy(
            src_ref=a, dst_ref=b, send_sem=small_sends.at[n], recv_sem=small_recvs.at[n],
            device_id=across(hop), device_id_type=MESH,
        )

    x, y = bit(ALONG_X), bit(ALONG_Y)
    slot_x, slot_y = 2 * y + 1 - x, 2 * (1 - y) + x
    smalls = [
        small_copy(0, small_ref, slots.at[me], ALONG_X),
        small_copy(1, small_ref, slots.at[me], ALONG_Y),
        small_copy(2, slots.at[slot_x, 0:8], slots.at[slot_x, 0:8], ALONG_Y),
        small_copy(3, slots.at[slot_y, 8:16], slots.at[slot_y, 8:16], ALONG_X),
    ]

    def conv_put(start, size):
        return lambda at, n: conv_full.at[rows_at(at, n), start : start + size]

    def gate_put(start, size):
        return lambda at, n: wg_full.at[rows_at(at, n), start : start + size]

    def out_put(start, size):
        return lambda at, n: wo_full.at[rows_at(at, n), start : start + size]

    sems = (sends, recvs)
    pieces = []
    for start, size in ((0, 768), (768, 768), (1536, 896)):
        pieces.append(weight_piece(
            stage_in, slice(D_INNER + start, D_INNER + start + size), conv_put(start, size), sems, len(pieces), rows_in))
    for start, size in ((0, 1024), (1024, 1024)):
        pieces.append(weight_piece(stage_in, slice(start, start + size), gate_put(start, size), sems, len(pieces), rows_in))
    for start, size in ((0, 512), (512, 512)):
        pieces.append(weight_piece(stage_out, slice(start, start + size), out_put(start, size), sems, len(pieces), rows_out))
    OWN, PASS, CORNER, ARRIVE, FINISH = range(5)

    def turn(start, count):
        def body(i, _):
            at = pl.ds(pl.multiple_of(start + i * LANES, LANES), LANES)
            stage_in[:, at] = wt_f32[at, :].T.astype(BF16)
            return 0

        lax.fori_loop(0, count, body, 0)

    @pl.when(j == 0)
    def _():
        load_conv.start()
        load_gate.start()
        load_out.start()
        wt_f32[STEP_AT + H : ALL] = jnp.zeros((LANES - H, wt_f32.shape[1]), F32)
        greet((CORE, ALONG_X, ALONG_Y))
        smalls[0].start()
        smalls[1].start()
        load_conv.wait()
        turn(D_INNER, 6)
        pieces[0][OWN]()
        smalls[0].wait_recv()
        smalls[2].start()
        smalls[1].wait_recv()
        smalls[3].start()
        slots[me] = small_ref[...]
        turn(D_INNER + 768, 6)
        pieces[1][OWN]()
        segment_masks(seg_ref, segb_ref, segpad, mask)
        pieces[0][PASS]()
        smalls[2].wait_recv()
        smalls[3].wait_recv()
        unpack_small(slots, taps_ref, vec_ref, hv_ref, skip_ref)
        turn(D_INNER + 1536, 7)
        keep_conv.start()
        pieces[0][CORNER]()
        pieces[2][OWN]()
        pieces[1][PASS]()
        norm_rows(tok_ref, vec_ref[0:1, :D], nrm_ref)
        keep_conv.wait()
        pieces[0][ARRIVE]()

    @pl.when(j == 1)
    def _():
        pieces[1][CORNER]()
        pieces[2][PASS]()
        load_gate.wait()
        turn(0, 16)
        keep_gate.start()
        pieces[3][OWN]()

    @pl.when(j == 3)
    def _():
        pieces[1][ARRIVE]()
        pieces[2][CORNER]()
        load_out.wait()

        def cast(i, _):
            at = pl.ds(pl.multiple_of(i * 32, 32), 32)
            stage_out[at] = wo_f32[at].astype(BF16)
            return 0

        lax.fori_loop(0, rows_out // 32, cast, 0)
        keep_out.start()
        pieces[4][OWN]()

    @pl.when(j == 4)
    def _():
        pieces[3][PASS]()

    @pl.when(j == 6)
    def _():
        pieces[2][ARRIVE]()
        write_conv.start()
        sraw_ref[...] = dot_nn(nrm_ref[...], conv_full[:, CONV_CH:])
        pieces[3][CORNER]()
        pieces[4][PASS]()
        pieces[5][OWN]()

    @pl.when(j == 8)
    def _():
        pieces[4][CORNER]()
        pieces[6][OWN]()

    @pl.when(j < CT)
    def _():
        conv_tile(j, nrm_ref, conv_full, taps_ref, vec_ref, mask, act_ref, dsilu_ref, cin_ref, pad)
        act[:, tile_at(j)] = act_ref[...]

    @pl.when(j == CT)
    def _():
        pieces[5][PASS]()

    @pl.when(j == CT + 1)
    def _():
        pieces[5][CORNER]()
        pieces[6][PASS]()

    @pl.when(j == CT + 2)
    def _():
        pieces[6][CORNER]()

    @pl.when(j >= CT)
    def _():
        scan_forward(j - CT, act, sraw_ref, segb_ref, seg_ref, hv_ref, skip_ref, y_ref, st_ref, scan)

    @pl.when(j == pl.num_programs(0) - 1)
    def _():
        for n in range(3, 7):
            pieces[n][ARRIVE]()
        for piece in pieces:
            piece[FINISH]()
        for one in smalls:
            one.wait_send()
        keep_gate.wait()
        keep_out.wait()
        write_conv.wait()


def plain_project_kernel(
    tok_ref, seg_ref, w_ref, slots,
    act_ref, dsilu_ref, cin_ref, y_ref, st_ref, sraw_ref, nrm_ref, segb_ref, taps_ref, vec_ref, hv_ref, skip_ref,
    pad, segpad, mask, act, *scan,
):
    j = pl.program_id(0)

    @pl.when(j == 0)
    def _():
        segment_masks(seg_ref, segb_ref, segpad, mask)
        unpack_small(slots, taps_ref, vec_ref, hv_ref, skip_ref)
        norm_rows(tok_ref, vec_ref[0:1, :D], nrm_ref)
        sraw_ref[...] = dot_nn(nrm_ref[...], w_ref[:, CONV_CH:])

    @pl.when(j < CT)
    def _():
        conv_tile(j, nrm_ref, w_ref, taps_ref, vec_ref, mask, act_ref, dsilu_ref, cin_ref, pad)
        act[:, tile_at(j)] = act_ref[...]

    @pl.when(j >= CT)
    def _():
        scan_forward(j - CT, act, sraw_ref, segb_ref, seg_ref, hv_ref, skip_ref, y_ref, st_ref, scan)


def project_outputs(length):
    col = lambda j: (0, jnp.minimum(j, CT - 1))
    fixed = lambda j: (0, 0)
    shapes = [((length, CONV_CH), BF16)] * 3 + [((length, D_INNER), F32), ((length // T, NSTATE, D_INNER), BF16)]
    specs = [pl.BlockSpec((length, W), col)] * 3 + [
        pl.BlockSpec((T, D_INNER), lambda j: (jnp.maximum(j - CT, 0), 0)),
        pl.BlockSpec((1, NSTATE, D_INNER), lambda j: (jnp.maximum(j - CT, 0), 0, 0)),
    ]
    for shape, dtype in (
        ((length, LANES), F32), ((length, D), BF16), ((length, LANES), F32), ((8, CONV_CH), F32), ((8, VEC_PAD), F32),
        ((8, LANES), F32), ((8, D_INNER), F32),
    ):
        shapes.append((shape, dtype))
        specs.append(pl.BlockSpec(shape, fixed))
    scratch = [
        pltpu.VMEM((8 + length, W), F32),
        pltpu.VMEM((8 + length, LANES), F32),
        pltpu.VMEM((KERNEL - 1, length, LANES), F32),
        pltpu.VMEM((length, CONV_CH), BF16),
        *scan_scratch(),
    ]
    return [jax.ShapeDtypeStruct(*one) for one in shapes], specs, scratch


def project_call(tok, seg, wt, wo, small):
    length = tok.shape[0]
    shapes, specs, scratch = project_outputs(length)
    hbm = pl.BlockSpec(memory_space=pl.ANY)
    shapes += [jax.ShapeDtypeStruct(shape, BF16) for shape in ((D, D_INNER), (D, CONV_CH + LANES), (D_INNER, D))]
    return pl.pallas_call(
        project_kernel,
        grid=(CT + length // T,),
        in_specs=[whole(tok.shape), whole(seg.shape), hbm, hbm, whole(small.shape)],
        out_specs=specs + [hbm] * 3,
        out_shape=shapes,
        scratch_shapes=[
            pltpu.VMEM((ALL, D // 4), F32),
            pltpu.VMEM((D_INNER // 4, D), F32),
            pltpu.VMEM((D // 4, ALL), BF16),
            pltpu.VMEM((D_INNER // 4, D), BF16),
            pltpu.VMEM((D, CONV_CH + LANES), BF16),
            pltpu.VMEM((4, *small.shape), F32),
            *scratch,
            pltpu.SemaphoreType.DMA((7,)),
            pltpu.SemaphoreType.DMA((7, 8)),
            pltpu.SemaphoreType.DMA((7, 8)),
            pltpu.SemaphoreType.DMA((4,)),
            pltpu.SemaphoreType.DMA((4,)),
        ],
        compiler_params=pltpu.CompilerParams(collective_id=0, has_side_effects=True, vmem_limit_bytes=VMEM_LIMIT),
        cost_estimate=pl.CostEstimate(flops=2 * length * D * CONV_CH, bytes_accessed=40 << 20, transcendentals=0),
    )(tok, seg, wt, wo, small)


def plain_project_call(tok, seg, w_conv, slots):
    length = tok.shape[0]
    shapes, specs, scratch = project_outputs(length)
    return pl.pallas_call(
        plain_project_kernel,
        grid=(CT + length // T,),
        in_specs=[whole(tok.shape), whole(seg.shape), whole(w_conv.shape), whole(slots.shape)],
        out_specs=specs,
        out_shape=shapes,
        scratch_shapes=scratch,
        compiler_params=pltpu.CompilerParams(vmem_limit_bytes=VMEM_LIMIT),
        cost_estimate=pl.CostEstimate(flops=2 * length * D * CONV_CH, bytes_accessed=20 << 20, transcendentals=0),
    )(tok, seg, w_conv, slots)


def fwd_kernel(
    xs_ref, y_ref, nrm_ref, tok_ref, cot_ref, wg_ref, wo_ref, vec_ref, skip_ref,
    out_ref, mixed_ref, gy_ref, gg_ref, rsum_ref, dgain_ref, dskip_ref,
    silu_scr, sig_scr, gated_scr, gm_scr, sums, rho_b, high, low, pick,
):
    block = pl.program_id(0)

    @pl.when(block == 0)
    def _():
        dgain_ref[...] = jnp.zeros_like(dgain_ref)
        dskip_ref[...] = jnp.zeros_like(dskip_ref)
        set_pick(pick)

    sums[...] = jnp.zeros_like(sums)

    def gate_product(i):
        cols = tile_of(i)
        silu_scr[:, cols] = dot_nn(nrm_ref[...], wg_ref[:, cols])

    gate_product(0)
    for i in range(NT):
        if i + 1 < NT:
            gate_product(i + 1)
        cols = tile_of(i)
        for rows in chunks():
            gate = silu_scr[rows, cols]
            sig = sigmoid(gate)
            silu = gate * sig
            sig_scr[rows, cols] = sig
            silu_scr[rows, cols] = silu
            gated = y_ref[rows, cols] * silu
            gated_scr[rows, cols] = gated
            g2 = gated * gated
            sums[rows] += g2[:, :LANES] + g2[:, LANES:]

    def mixed_product(i):
        cols = tile_of(i)
        gm_scr[:, cols] = dot_nt(cot_ref[...], wo_ref[cols, :])

    mixed_product(0)
    mean2 = jnp.sum(sums[...], axis=1, keepdims=True) * (1.0 / D_INNER)
    rho_b[...] = jnp.broadcast_to(lax.rsqrt(mean2 + EPSILON), (T, LANES))
    sums[...] = jnp.zeros_like(sums)

    for i in range(NT):
        if i + 1 < NT:
            mixed_product(i + 1)
        cols = tile_of(i)
        gain = vec_ref[0:1, D + i * W : D + (i + 1) * W]
        total = jnp.zeros((8, W), F32)
        for rows in chunks():
            gated = gated_scr[rows, cols]
            unit = gated * wide(rho_b[rows])
            mixed_ref[rows, cols] = (unit * gain).astype(BF16)
            gm = gm_scr[rows, cols]
            total = total + rows8(gm * unit)
            e = gm * gain
            gm_scr[rows, cols] = e
            eg = e * gated
            sums[rows] += eg[:, :LANES] + eg[:, LANES:]
        dgain_ref[:, cols] += total

    rho = rho_b[...]
    inner = jnp.sum(sums[...], axis=1, keepdims=True) * (1.0 / D_INNER)
    sums[...] = inner * rho * rho * rho
    rsum_ref[...] = jnp.zeros_like(rsum_ref)

    def out_product(j):
        cols = tile_of(j)
        branch = dot_nn(mixed_ref[...], wo_ref[:, cols])
        out_ref[:, cols] = (tok_ref[:, cols].astype(F32) + branch).astype(BF16)

    for i in range(NT):
        if i % 2 == 0:
            out_product(i // 2)
        cols = tile_of(i)
        skip = skip_ref[0:1, cols]
        total = jnp.zeros((8, W), F32)
        p = i % 2
        for rows in chunks():
            sig = sig_scr[rows, cols]
            silu = silu_scr[rows, cols]
            y = y_ref[rows, cols]
            grad_gated = wide(rho_b[rows]) * gm_scr[rows, cols] - gated_scr[rows, cols] * wide(sums[rows])
            gg_ref[rows, cols] = (grad_gated * y * (sig + silu * (1.0 - sig))).astype(BF16)
            gy = (grad_gated * silu).astype(BF16)
            gy_ref[rows, cols] = gy
            gy = gy.astype(F32)
            xs = xs_ref[rows, cols].astype(F32)
            total = total + rows8(gy * xs)
            split_halves(gy * (y - xs * skip), high.at[p], low.at[p], rows)
        dskip_ref[:, cols] += total
        rsum_ref[...] += head_sums(high.at[p], low.at[p], pick[cols, :])


def fwd_call(xs_bc, y, nrm, tok, cot, wg, wo, vec, skip):
    length = nrm.shape[0]
    blocks = length // T
    tokens = lambda b: (b, 0)
    fixed = lambda b: (0, 0)
    wide_block = pl.BlockSpec((T, D_INNER), tokens)
    return pl.pallas_call(
        fwd_kernel,
        grid=(blocks,),
        in_specs=[
            wide_block,
            wide_block,
            pl.BlockSpec((T, D), tokens),
            pl.BlockSpec((T, D), tokens),
            pl.BlockSpec((T, D), tokens),
            whole(wg.shape),
            whole(wo.shape),
            whole(vec.shape),
            whole(skip.shape),
        ],
        out_specs=[
            pl.BlockSpec((T, D), tokens),
            wide_block,
            wide_block,
            wide_block,
            pl.BlockSpec((T, LANES), tokens),
            pl.BlockSpec((8, D_INNER), fixed),
            pl.BlockSpec((8, D_INNER), fixed),
        ],
        out_shape=[
            jax.ShapeDtypeStruct((length, D), BF16),
            jax.ShapeDtypeStruct((length, D_INNER), BF16),
            jax.ShapeDtypeStruct((length, D_INNER), BF16),
            jax.ShapeDtypeStruct((length, D_INNER), BF16),
            jax.ShapeDtypeStruct((length, LANES), F32),
            jax.ShapeDtypeStruct((8, D_INNER), F32),
            jax.ShapeDtypeStruct((8, D_INNER), F32),
        ],
        scratch_shapes=[
            pltpu.VMEM((T, D_INNER), F32),
            pltpu.VMEM((T, D_INNER), F32),
            pltpu.VMEM((T, D_INNER), F32),
            pltpu.VMEM((T, D_INNER), F32),
            pltpu.VMEM((T, LANES), F32),
            pltpu.VMEM((T, LANES), F32),
            pltpu.VMEM((2, T, W), BF16),
            pltpu.VMEM((2, T, W), BF16),
            pltpu.VMEM((D_INNER, LANES), BF16),
        ],
        compiler_params=pltpu.CompilerParams(vmem_limit_bytes=VMEM_LIMIT),
        cost_estimate=pl.CostEstimate(flops=2 * length * D * D_INNER * 3, bytes_accessed=40 << 20, transcendentals=0),
    )(xs_bc, y, nrm, tok, cot, wg, wo, vec, skip)


def bwd_kernel(remote, *refs):
    if remote:
        ticks, ends, refs = gate_out_plan(refs)
        slots = by_slot(ticks)
    (
        xs_ref, bc_ref, sraw_ref, segb_ref, seg_ref, prev_ref, gy_ref, st_ref, rsum_ref, dsilu_ref, cin_ref,
        hv_ref, skip_ref, taps_ref,
        gc_ref, dtaps_ref, dhv_ref,
        gstate, cum_b, fan, wcat, cum_rows, gf, gscore, gyw_scr, xw_scr, back_scr, through, diag_x, diag_y, gw_scr, gx_scr,
        scores, x1_scr, high, low, high_s, pick, segpad, mask, inner_ref, outer_ref, step_f, from_start, to_end,
    ) = refs
    turn = pl.program_id(0)
    last_turn = pl.num_programs(0) - 1

    @pl.when(turn == 0)
    def _():
        gstate[...] = jnp.zeros_like(gstate)
        wcat[...] = jnp.zeros_like(wcat)
        diag_x[...] = jnp.zeros_like(diag_x)
        diag_y[...] = jnp.zeros_like(diag_y)
        dtaps_ref[...] = jnp.zeros_like(dtaps_ref)
        dhv_ref[...] = jnp.zeros_like(dhv_ref)
        gf[T : T + 8] = jnp.zeros((8, CONV_CH), F32)
        segpad[T : T + 8] = jnp.full((8, LANES), -1.0, F32)
        set_pick(pick)
        set_fan(fan)
        if remote:
            greet(range(5))

    @pl.when(turn > 0)
    def _():
        gf[T : T + 8] = gf[0:8]
        segpad[T : T + 8] = segpad[0:8]

    segb = segb_ref[...]
    segpad[0:T] = segb
    for k in range(1, KERNEL):
        mask[k - 1] = jnp.where(segpad[k : k + T] == segb, 1.0, 0.0)
    v, step, rate = head_terms(sraw_ref, hv_ref)
    logdecay = step * rate
    cum = cumulate(logdecay)
    cum_rows[...] = cum.T
    spread(cum, cum_b)
    bmat = bc_ref[:, :NSTATE]
    cmat = bc_ref[:, NSTATE:]
    s_at, t_at = before(T, T)
    same = wide(segb) == seg_ref[...].astype(F32)
    valid = same & (s_at <= t_at)
    scores[...] = jnp.where(valid, dot_nt(bmat, cmat), 0.0).astype(BF16)
    prev = jnp.where(turn == last_turn, -1.0, prev_ref[7:8])
    last_seg = segb[T - 1 : T]
    last = cum[T - 1 : T]
    expand(step, fan, step_f)
    expand(jnp.exp2(cum) * jnp.where(segb == prev, 1.0, 0.0), fan, from_start)
    expand(jnp.exp2(last - cum) * jnp.where(segb == last_seg, 1.0, 0.0), fan, to_end)
    keep = wide(jnp.where(last_seg == prev, 1.0, 0.0))
    c_t = cmat.astype(F32).T.astype(BF16)
    gst_b = gstate[...].astype(BF16)
    back_scr[...] = dot_nn(bmat, gst_b)
    gscore[...] = jnp.zeros_like(gscore)
    inner_ref[...] = jnp.zeros_like(inner_ref)
    outer_ref[...] = jnp.zeros_like(outer_ref)

    def spread_out(i, p):
        cols = tile_at(i)
        for rows in chunks():
            x1 = (xs_ref[rows, cols].astype(F32) * step_f[rows, cols]).astype(BF16)
            x1_scr[p, rows] = x1
            put_diagonal(diag_x.at[p], rows.start, x1)
            gy = gy_ref[rows, cols]
            put_diagonal(diag_y.at[p], rows.start, gy)
            xw_scr[rows, cols] = (x1.astype(F32) * to_end[rows, cols]).astype(BF16)
            gyw_scr[rows, cols] = (gy.astype(F32) * from_start[rows, cols]).astype(BF16)

    def pair_product(i, p):
        gw_scr[p] = dot_nt(diag_x[p], gy_ref[:, tile_at(i)])

    def decays(i, p):
        for rows in chunks():
            start = 0 if rows.start < LANES else LANES
            total = gscore[rows, start:]
            score = scores[rows, start:]
            for k in range(HPT):
                row = cum_rows[pl.ds(HPT * i + k, 1), :]
                colb = cum_b[HPT * i + k, rows]
                colb = colb if start else wide(colb)
                decay = jnp.exp2(jnp.minimum(row[:, start:] - colb, 0.0))
                wcat[p, rows, k * T + start : (k + 1) * T] = score * decay.astype(BF16)
                total = total + gw_scr[p, k * T + rows.start : k * T + rows.stop, start:] * decay
            gscore[rows, start:] = total

    def grad_product(p):
        gx_scr[p] = dot_nn(wcat[p], diag_y[p])

    def collect(i, p):
        cols = tile_at(i)
        skip = skip_ref[0:1, cols]
        for rows in chunks():
            gx1 = gx_scr[p, rows]
            x1 = x1_scr[p, rows].astype(F32)
            from_state = back_scr[rows, cols] * to_end[rows, cols]
            split_halves(x1 * gx1, high.at[p], low.at[p], rows)
            high_s[p, rows] = (x1 * from_state).astype(BF16)
            gx = (gx1 + from_state) * step_f[rows, cols] + gy_ref[rows, cols].astype(F32) * skip
            gf[rows, cols] = gx * dsilu_ref[rows, cols].astype(F32)
        fade = from_start_last(cum_b, i) * keep
        total = jnp.zeros((8, W), F32)
        for rows in chunks(0, NSTATE):
            gst = gstate[rows, cols] * fade
            gstate[rows, cols] = gst
            total = total + rows8(gst * st_ref[0, rows, cols].astype(F32))
        through[:, cols] = total

    def head_product(i, p):
        pick_i = pick[tile_at(i), :]
        inner_ref[...] += head_sums(high.at[p], low.at[p], pick_i)
        outer_ref[...] += dot_nn(high_s[p], pick_i)

    def two_groups(n, _):
        a, b = 2 * n, 2 * n + 1
        spread_out(a, 0)
        pair_product(a, 0)
        spread_out(b, 1)
        pair_product(b, 1)
        decays(a, 0)
        grad_product(0)
        decays(b, 1)
        grad_product(1)
        collect(a, 0)
        head_product(a, 0)
        collect(b, 1)
        head_product(b, 1)
        if remote:
            for slot, actions in slots.items():

                @pl.when(turn * NT + a == slot - slot % 2)
                def _():
                    for action in actions:
                        action()

        return 0

    lax.fori_loop(0, NT // 2, two_groups, 0)
    gyw = gyw_scr[...]
    gstate[...] += dot_nn(c_t, gyw)
    gsc = jnp.where(valid, gscore[...], 0.0)
    g_b = dot_nn(gsc.astype(BF16), cmat) + dot_nt(xw_scr[...], gst_b)
    g_c = dot_nn(gsc.T.astype(BF16), bmat) + dot_nt(gyw, st_ref[0])
    tail_cols = slice(D_INNER, CONV_CH)
    gf[0:T, tail_cols] = jnp.concatenate([g_b, g_c], axis=1) * dsilu_ref[:, tail_cols].astype(F32)

    inner_sum, outer_sum = inner_ref[...], outer_ref[...]
    after = jnp.where(valid, 1.0, 0.0)
    ahead = jnp.where(same & (s_at > t_at), 1.0, 0.0)
    flow = through[...]
    flow_high = flow.astype(BF16)
    flow_low = (flow - flow_high.astype(F32)).astype(BF16)
    over = jnp.sum(dot_nn(flow_high, pick[...]) + dot_nn(flow_low, pick[...]), axis=0, keepdims=True)
    gl = jnp.dot(after, rsum_ref[...] - inner_sum, precision=HIGHEST, preferred_element_type=F32)
    gl = gl + jnp.dot(ahead, outer_sum, precision=HIGHEST, preferred_element_type=F32) + over
    grad_step = (inner_sum + outer_sum) / jnp.maximum(step, 1e-37) + gl * rate
    lane = lax.broadcasted_iota(jnp.int32, (T, LANES), 1)
    g_sraw = jnp.where(lane < H, grad_step * sigmoid(v), 0.0)
    gc_ref[:, CONV_CH:] = g_sraw.astype(BF16)
    dhv_ref[0:8] += rows8(g_sraw)
    dhv_ref[8:16] += rows8(gl * logdecay)

    def conv_group(j, _):
        cols = tile_at(j)
        taps = [taps_ref[k : k + 1, cols] for k in range(KERNEL)]
        totals = [jnp.zeros((8, W), F32) for _ in range(KERNEL + 1)]
        for rows in chunks():
            here = gf[rows, cols]
            cin = cin_ref[rows, cols].astype(F32)
            totals[KERNEL] = totals[KERNEL] + rows8(here)
            totals[0] = totals[0] + rows8(cin * here)
            total = here * taps[0]
            for k in range(1, KERNEL):
                u = gf[rows.start + k : rows.stop + k, cols] * wide(mask[k - 1, rows])
                total = total + u * taps[k]
                totals[k] = totals[k] + rows8(cin * u)
            gc_ref[rows, cols] = total.astype(BF16)
        for k in range(KERNEL + 1):
            dtaps_ref[8 * k : 8 * k + 8, cols] += totals[k]
        return 0

    lax.fori_loop(0, CT, conv_group, 0)

    if remote:

        @pl.when(turn == last_turn)
        def _():
            for end in ends:
                end()


OUT_CHUNKS, GATE_CHUNKS = 4, 4
OUT_COLS, GATE_COLS = D // OUT_CHUNKS, D_INNER // GATE_CHUNKS
BWD_PACE = (0, 4, 8, 10, 12, 14, 16, 18, 20)
BWD_SLOTS = (0, 1, 3, 4, 6, 7, 9, 11)
TOKEN_PACE = (0, 2, 4, 6, 7, 8, 9, 10, 11)


def gate_out_plan(refs):
    ins, outs, scratch = 14, 3, 28
    head, rest = refs[:ins], refs[ins:]
    (grad_out, grad_gate), rest = rest[:2], rest[2:]
    mid, rest = rest[:outs], rest[outs:]
    (out_total, gate_total), rest = rest[:2], rest[2:]
    tail, rest = rest[:scratch], rest[scratch:]
    out_bufs, gate_bufs, sems = rest[:BUFFERS], rest[BUFFERS : 2 * BUFFERS], rest[2 * BUFFERS :]
    out_starts = [OUT_COLS * n for n in range(OUT_CHUNKS)]
    gate_starts = [GATE_COLS * n for n in range(GATE_CHUNKS)]
    ticks, ends = reduce_plan(
        grad_out, out_starts, OUT_COLS, BWD_SLOTS[0::2], BWD_PACE, out_bufs, out_total, sems, 0, [True] * OUT_CHUNKS
    )
    more, more_ends = reduce_plan(
        grad_gate, gate_starts, GATE_COLS, BWD_SLOTS[1::2], BWD_PACE, gate_bufs, gate_total, sems, OUT_CHUNKS,
        [False] * GATE_CHUNKS,
    )
    return ticks + more, ends + more_ends, (*head, *mid, *tail)


def reduce_sems(count):
    return [
        pltpu.SemaphoreType.DMA((count,)),
        pltpu.SemaphoreType.DMA((count,)),
        pltpu.SemaphoreType.DMA((count, 8)),
        pltpu.SemaphoreType.DMA((count, 8)),
    ]


def bwd_call(xs_bc, sraw, segb, seg, gy, states, rsum, dsilu, cin, hv, skip, taps, grad_out=None, grad_gate=None):
    remote = grad_out is not None
    hbm = pl.BlockSpec(memory_space=pl.ANY)
    length = gy.shape[0]
    blocks = length // T
    tokens = lambda b: (blocks - 1 - b, 0)
    third = lambda b: (blocks - 1 - b, 0, 0)
    fixed = lambda b: (0, 0)
    return pl.pallas_call(
        functools.partial(bwd_kernel, remote),
        grid=(blocks,),
        in_specs=[
            pl.BlockSpec((T, D_INNER), tokens),
            pl.BlockSpec((T, 2 * NSTATE), lambda b: (blocks - 1 - b, D_INNER // (2 * NSTATE))),
            pl.BlockSpec((T, LANES), tokens),
            pl.BlockSpec((T, LANES), tokens),
            pl.BlockSpec((1, T), lambda b: (0, blocks - 1 - b)),
            pl.BlockSpec((8, LANES), lambda b: (jnp.maximum((blocks - 1 - b) * (T // 8) - 1, 0), 0)),
            pl.BlockSpec((T, D_INNER), tokens),
            pl.BlockSpec((1, NSTATE, D_INNER), third),
            pl.BlockSpec((T, LANES), tokens),
            pl.BlockSpec((T, CONV_CH), tokens),
            pl.BlockSpec((T, CONV_CH), tokens),
            whole(hv.shape),
            whole(skip.shape),
            whole(taps.shape),
            *([hbm] * 2 if remote else []),
        ],
        out_specs=[
            pl.BlockSpec((T, CONV_CH + LANES), tokens),
            pl.BlockSpec((8 * (KERNEL + 1), CONV_CH), fixed),
            pl.BlockSpec((16, LANES), fixed),
            *([hbm] * 2 if remote else []),
        ],
        out_shape=[
            jax.ShapeDtypeStruct((length, CONV_CH + LANES), BF16),
            jax.ShapeDtypeStruct((8 * (KERNEL + 1), CONV_CH), F32),
            jax.ShapeDtypeStruct((16, LANES), F32),
            *([jax.ShapeDtypeStruct(g.shape[2:], BF16) for g in (grad_out, grad_gate)] if remote else []),
        ],
        scratch_shapes=[
            pltpu.VMEM((NSTATE, D_INNER), F32),
            pltpu.VMEM((H, T, LANES), F32),
            pltpu.VMEM((2 * LANES, D_INNER), BF16),
            pltpu.VMEM((2, T, HPT * T), BF16),
            pltpu.VMEM((LANES, T), F32),
            pltpu.VMEM((T + 8, CONV_CH), F32),
            pltpu.VMEM((T, T), F32),
            pltpu.VMEM((T, D_INNER), BF16),
            pltpu.VMEM((T, D_INNER), BF16),
            pltpu.VMEM((T, D_INNER), F32),
            pltpu.VMEM((8, D_INNER), F32),
            pltpu.VMEM((2, HPT * T, W), BF16),
            pltpu.VMEM((2, HPT * T, W), BF16),
            pltpu.VMEM((2, HPT * T, T), F32),
            pltpu.VMEM((2, T, W), F32),
            pltpu.VMEM((T, T), BF16),
            pltpu.VMEM((2, T, W), BF16),
            pltpu.VMEM((2, T, W), BF16),
            pltpu.VMEM((2, T, W), BF16),
            pltpu.VMEM((2, T, W), BF16),
            pltpu.VMEM((D_INNER, LANES), BF16),
            pltpu.VMEM((T + 8, LANES), F32),
            pltpu.VMEM((KERNEL - 1, T, LANES), F32),
            pltpu.VMEM((T, LANES), F32),
            pltpu.VMEM((T, LANES), F32),
            pltpu.VMEM((T, D_INNER), F32),
            pltpu.VMEM((T, D_INNER), F32),
            pltpu.VMEM((T, D_INNER), F32),
            *(
                reduce_buffers(grad_out.shape[2], OUT_COLS, OUT_CHUNKS)
                + reduce_buffers(grad_gate.shape[2], GATE_COLS, GATE_CHUNKS)
                + reduce_sems(OUT_CHUNKS + GATE_CHUNKS)
                if remote
                else []
            ),
        ],
        compiler_params=pltpu.CompilerParams(
            vmem_limit_bytes=VMEM_LIMIT, **(dict(collective_id=1, has_side_effects=True) if remote else {})
        ),
        cost_estimate=pl.CostEstimate(flops=2 * length * D * D_INNER * 4, bytes_accessed=30 << 20, transcendentals=0),
    )(xs_bc, xs_bc, sraw, segb, seg, segb, gy, states, rsum, dsilu, cin, hv, skip, taps, *((grad_out, grad_gate) if remote else ()))


CONV_COLS = 2 * W
CONV_CHUNKS = (CONV_CH + LANES) // CONV_COLS
CONV_DONE = CONV_CHUNKS * CONV_COLS
CONV_LEFT = CONV_CH + LANES - CONV_DONE


def token_kernel(remote, *refs):
    (gg_ref, gc_ref, wg_hbm, wc_hbm, tok_ref, cot_ref, vec_ref, taps_sum, vec_sum), refs = refs[:9], refs[9:]
    if remote:
        grad_conv, refs = refs[0], refs[1:]
        (tg_ref, small_total, conv_total), refs = refs[:3], refs[3:]
    else:
        (tg_ref, small_total), refs = refs[:2], refs[2:]
    (wg, wc, grad, dpre, small, load_sems), refs = refs[:6], refs[6:]
    turn = pl.program_id(0)
    last_turn = pl.num_programs(0) - 1
    loads = [
        pltpu.make_async_copy(wg_hbm, wg, load_sems.at[0]),
        pltpu.make_async_copy(wc_hbm, wc, load_sems.at[1]),
    ]
    pieces = D // CONV_COLS
    slots = {}
    if remote:
        conv_bufs, step_bufs, refs = refs[:BUFFERS], refs[BUFFERS : 2 * BUFFERS], refs[2 * BUFFERS :]
        small_bufs, refs = refs[:9], refs[9:]
        sems, small_sems = refs[:4], refs[4:]
        starts = [CONV_COLS * n for n in range(CONV_CHUNKS)]
        ticks, ends = reduce_plan(
            grad_conv, starts, CONV_COLS, range(CONV_CHUNKS), TOKEN_PACE, conv_bufs, conv_total, sems, 0,
            [n % 2 == 0 for n in range(CONV_CHUNKS)],
        )
        more, more_ends = reduce_plan(
            grad_conv, [CONV_DONE], CONV_LEFT, [CONV_CHUNKS], TOKEN_PACE, step_bufs, conv_total, sems, CONV_CHUNKS,
            [True],
        )
        done = 4 * pieces
        last, last_ends = small_plan(small, small_bufs, small_total, small_sems, done, 1)
        slots = by_slot(ticks + more + last)
        ends = ends + more_ends + last_ends

    @pl.when(turn == 0)
    def _():
        for load in loads:
            load.start()
        dpre[...] = jnp.zeros_like(dpre)
        if remote:
            greet(range(5))
            for action in slots.pop(0):
                action()
        for load in loads:
            load.wait()

    def piece(q, _):
        rows = tile_at(q, CONV_COLS)
        grad[:, rows] = dot_nt(gg_ref[...], wg[rows, :]) + dot_nt(gc_ref[...], wc[rows, :])
        for slot, actions in slots.items():
            if slot < 4 * pieces:

                @pl.when(turn * pieces + q == slot)
                def _():
                    for action in actions:
                        action()

        return 0

    lax.fori_loop(0, pieces, piece, 0)
    gain = vec_ref[0:1, :D]
    total = jnp.zeros((8, D), F32)
    step = 16
    for r in range(0, T, step):
        rows = slice(r, r + step)
        tok = tok_ref[rows].astype(F32)
        rho = lax.rsqrt(jnp.sum(tok * tok, axis=1, keepdims=True) * (1.0 / D) + EPSILON)
        unit = tok * rho
        g = grad[rows]
        total = total + rows8(g * unit)
        e = g * gain
        mean = jnp.sum(e * unit, axis=1, keepdims=True) * (1.0 / D)
        tg_ref[rows] = cot_ref[rows].astype(F32) + rho * (e - unit * mean)
    dpre[...] += total

    @pl.when(turn == last_turn)
    def _():
        vec_sum_all = vec_sum[0:1, :]
        pre = jnp.sum(dpre[...], axis=0, keepdims=True)
        vec_all = jnp.concatenate([pre, vec_sum_all[:, D:]], axis=1)
        parts = small.shape[0] * small.shape[1] if remote else small.shape[0]
        n, m = CONV_CH // parts, VEC // parts
        small[...] = jnp.zeros_like(small)
        for p in range(parts):
            at = (p // 2, p % 2) if remote else (p,)
            small[(*at, slice(0, KERNEL), slice(0, n))] = taps_sum[0:KERNEL, n * p : n * (p + 1)]
            small[(*at, slice(8, 9), slice(0, m))] = vec_all[:, m * p : m * (p + 1)]
        if remote:
            for slot in sorted(slots):
                if slot >= 4 * pieces:
                    for action in slots[slot]:
                        action()
            for end in ends:
                end()
        else:
            small_total[...] = small[...]


def token_call(gg, gc, wg, wc, tok, cot, vec, taps_sum, vec_sum, parts, grad_conv=None):
    remote = grad_conv is not None
    length = tok.shape[0]
    tokens = lambda b: (b, 0)
    hbm = pl.BlockSpec(memory_space=pl.ANY)
    small = (2, 2, 16, SMALL_COLS) if remote else (parts, 16, SMALL_COLS)
    small_out = small[2:] if remote else small
    zeros = (0,) * len(small_out)
    return pl.pallas_call(
        functools.partial(token_kernel, remote),
        grid=(length // T,),
        in_specs=[
            pl.BlockSpec((T, D_INNER), tokens),
            pl.BlockSpec((T, CONV_CH + LANES), tokens),
            hbm,
            hbm,
            pl.BlockSpec((T, D), tokens),
            pl.BlockSpec((T, D), tokens),
            whole(vec.shape),
            whole(taps_sum.shape),
            whole(vec_sum.shape),
            *([hbm] if remote else []),
        ],
        out_specs=[
            pl.BlockSpec((T, D), tokens),
            pl.BlockSpec(small_out, lambda b: zeros),
            *([hbm] if remote else []),
        ],
        out_shape=[
            jax.ShapeDtypeStruct((length, D), F32),
            jax.ShapeDtypeStruct(small_out, F32),
            *([jax.ShapeDtypeStruct(grad_conv.shape[2:], BF16)] if remote else []),
        ],
        scratch_shapes=[
            pltpu.VMEM(wg.shape, BF16),
            pltpu.VMEM(wc.shape, BF16),
            pltpu.VMEM((T, D), F32),
            pltpu.VMEM((8, D), F32),
            pltpu.VMEM(small, F32),
            pltpu.SemaphoreType.DMA((2,)),
            *(
                reduce_buffers(grad_conv.shape[2], CONV_COLS, CONV_CHUNKS)
                + reduce_buffers(grad_conv.shape[2], CONV_LEFT, 1)
                + small_buffers(16, SMALL_COLS)
                + reduce_sems(CONV_CHUNKS + 1)
                + [pltpu.SemaphoreType.DMA((5,)), pltpu.SemaphoreType.DMA((5,))]
                if remote
                else []
            ),
        ],
        compiler_params=pltpu.CompilerParams(
            vmem_limit_bytes=VMEM_LIMIT, **(dict(collective_id=2, has_side_effects=True) if remote else {})
        ),
        cost_estimate=pl.CostEstimate(flops=2 * length * D * 4480, bytes_accessed=22 << 20, transcendentals=0),
    )(gg, gc, wg, wc, tok, cot, vec, taps_sum, vec_sum, *((grad_conv,) if remote else ()))


def adam_step(master, first, second, grad, rate):
    first_new = BETA_FIRST * first + (1.0 - BETA_FIRST) * grad
    second_new = BETA_SECOND * second + (1.0 - BETA_SECOND) * grad * grad
    first_fix = 1.0 - BETA_FIRST**STEP
    second_fix = 1.0 - BETA_SECOND**STEP
    master_new = master - rate * (
        first_new / first_fix / (jnp.sqrt(second_new / second_fix) + ADAM_EPSILON) + WEIGHT_DECAY * master
    )
    return (master_new, first_new, second_new)


def adam_rows(rate, grad, refs, rows):
    ins, outs = refs
    for ref, value in zip(outs, adam_step(*(r[rows] for r in ins), grad, rate)):
        ref[rows] = value


def adam_turned_kernel(rate, tiles, first_ref, second_ref, *refs):
    j = pl.program_id(0)
    for which, grad_ref in enumerate((first_ref, second_ref)):

        @pl.when((j >= tiles) == bool(which))
        def _():
            for r in range(0, 2 * W, LANES):
                rows = slice(r, r + LANES)
                adam_rows(rate, grad_ref[:, rows].astype(F32).T, (refs[:3], refs[3:]), rows)


def adam_kernel(rate, grad_ref, *refs):
    for r in range(0, refs[0].shape[0], 32):
        rows = slice(r, r + 32)
        adam_rows(rate, grad_ref[rows].astype(F32), (refs[:3], refs[3:]), rows)


def adam_call(grads, master, first, second, rate):
    rows, cols = master.shape
    if len(grads) == 2:
        tile = 2 * W
        tiles = grads[0].shape[1] // tile
        kernel = functools.partial(adam_turned_kernel, rate, tiles)
        grad_specs = [
            pl.BlockSpec((cols, tile), lambda j: (0, jnp.minimum(j, tiles - 1))),
            pl.BlockSpec((cols, tile), lambda j: (0, jnp.maximum(j - tiles, 0))),
        ]
    else:
        tile = rows // 4
        kernel = functools.partial(adam_kernel, rate)
        grad_specs = [pl.BlockSpec((tile, cols), lambda j: (j, 0))]
    down = pl.BlockSpec((tile, cols), lambda j: (j, 0))
    return pl.pallas_call(
        kernel,
        grid=(-(-rows // tile),),
        in_specs=[*grad_specs, down, down, down],
        out_specs=[down] * 3,
        out_shape=[jax.ShapeDtypeStruct((rows, cols), F32)] * 3,
        compiler_params=pltpu.CompilerParams(vmem_limit_bytes=VMEM_LIMIT),
        cost_estimate=pl.CostEstimate(flops=0, bytes_accessed=26 * rows * cols, transcendentals=0),
    )(*grads, master, first, second)


def owners(grad, parts, remote):
    return grad.reshape(*((2, 2) if remote else (parts,)), -1, grad.shape[1])


def row_pass(projected, tok, cot, seg, wg, wc, wo, parts, remote):
    act, dsilu, cin, y, states, sraw, nrm, segb, taps, vec, hv, skip = projected
    block_out, mixed, gy, gg, rsum, dgain, dskip = fwd_call(act, y, nrm, tok, cot, wg, wo, vec, skip)
    grad_out = owners(dot_tn(mixed, cot).astype(BF16), parts, remote)
    grad_gate = owners(dot_tn(nrm, gg).astype(BF16), parts, remote)
    gc, dtaps, dhv, *totals = bwd_call(
        act, sraw, segb, seg, gy, states, rsum, dsilu, cin, hv, skip, taps, *((grad_out, grad_gate) if remote else ())
    )
    grad_conv = owners(dot_tn(nrm, gc).astype(BF16), parts, remote)
    dtaps = dtaps.reshape(KERNEL + 1, 8, CONV_CH).sum(1)
    dhv = dhv.reshape(2, 8, LANES).sum(1)
    vec_sum = jnp.concatenate(
        [
            jnp.zeros((D,), F32),
            dgain.sum(0),
            dtaps[KERNEL],
            dhv[0, :H],
            dhv[1, :H],
            dskip.sum(0).reshape(H, P_SIZE).sum(1),
            jnp.zeros((VEC_PAD - VEC,), F32),
        ]
    )[None]
    token_grad, small, *conv_total = token_call(
        gg, gc, wg, wc, tok, cot, vec, dtaps, vec_sum, parts, *((grad_conv,) if remote else ())
    )
    if remote:
        out_total, gate_total = totals
        return block_out, token_grad, gate_total, conv_total[0], out_total, small
    return block_out, token_grad, grad_gate, grad_conv, grad_out, small


def local(
    tokens, cotangent, segment_ids, in_weight, out_weight, filter_weight, vectors,
    in_first, out_first, filter_first, vector_first, in_second, out_second, filter_second, vector_second,
):
    remote = lax.axis_size("grp") == 4 and lax.axis_size("dp") == 8
    parts = D // in_weight.shape[0]
    vec_size = vectors.size
    in_turned = in_weight.T
    small = jnp.pad(filter_weight, ((0, 12), (0, SMALL_COLS - filter_weight.shape[1])))
    small = small.at[8, :vec_size].set(vectors)
    tok, cot = tokens[0], cotangent[0]
    if remote:
        *projected, wg, wc, wo = project_call(tok, segment_ids, in_turned, out_weight, small)
    else:
        in_full = lax.all_gather(in_weight.astype(BF16), "grp", axis=0, tiled=True)
        wo = lax.all_gather(out_weight.astype(BF16), "grp", axis=0, tiled=True)
        slots = lax.all_gather(small, "grp")
        wg = in_full[:, :D_INNER]
        wc = jnp.pad(in_full[:, D_INNER:], ((0, 0), (0, LANES - H)))
        projected = plain_project_call(tok, segment_ids, wc, slots)
    block_out, token_grad, *grads = row_pass(projected, tok, cot, segment_ids, wg, wc, wo, parts, remote)
    if not remote:
        grads = [lax.psum(lax.psum_scatter(g, "grp", scatter_dimension=0, tiled=False), "dp") for g in grads]
    gate_total, conv_total, out_total, small_total = grads
    in_new = [a.T for a in adam_call((gate_total, conv_total), in_turned, in_first.T, in_second.T, 0.03)]
    out_new = adam_call((out_total,), out_weight, out_first, out_second, 0.02)
    filter_new = adam_step(
        filter_weight, filter_first, filter_second, small_total[:KERNEL, : filter_weight.shape[1]], 0.3
    )
    vector_new = adam_step(vectors, vector_first, vector_second, small_total[8, :vec_size], 0.3)
    results = (in_new, out_new, filter_new, vector_new)
    return (block_out[None], token_grad[None], *(r[n] for n in range(3) for r in results))


def solution(mesh):
    rows = P(("grp", "dp"), None, None)
    shards = (P("grp", None), P("grp", None), P(None, "grp"), P("grp"))
    in_specs = (rows, rows, P(("grp", "dp"), None)) + shards * 3
    out_specs = (rows, rows) + shards * 3
    return jax.shard_map(local, mesh=mesh, in_specs=in_specs, out_specs=out_specs, check_vma=False)
```

time: 1000 us -> 334 us (0.33); the launches traced: 986 us -> 333 us
  waiting for transfers between devices: 329 us -> 0 us
  Pallas kernels: 0 us -> 299 us
  matrix products: 314 us -> 24.5 us
  other arithmetic: 168 us -> 2.26 us
  local copies, waits for them, and re-layouts: 99.4 us -> 6.23 us
  blocking collectives: 59.3 us -> 0 us
  between operations: 17 us -> 0.91 us
    pallas_call x0 -> x6, Pallas kernels: none -> 299 us  [the longest x1 99.8 us: bwd_call(): pl.pallas_call(functools.partial(bwd_kernel, remote), grid=(blocks,), in_...]
    dot_general x18 -> x3, matrix products: 314 us -> 24.5 us  [dot_tn(): lax.dot_general(a, b, (((0,), (0,)), ((), ())), preferred_element_type=F32)]
    reduce_scatter x2 -> x0, waiting for transfers between devices: 161 us -> none  [the longest x1 161 us: local(): lax.psum_scatter(grad_in, 'grp', scatter_dimension=0, tiled=True)]
    psum x1 -> x0, waiting for transfers between devices: 102 us -> none  [local(): lax.psum((in_share, out_share, filter_share, vector_share), 'dp')]
    reduce_sum x13 -> x5, other arithmetic: 69.5 us -> 0.28 us  [the longest x2 0.14 us: row_pass(): dskip.sum(0).reshape(H, P_SIZE).sum(1)]
    all_gather x2 -> x0, waiting for transfers between devices: 65.8 us -> none  [the longest x1 65.8 us: local(): lax.all_gather(in_weight.astype(jnp.bfloat16), 'grp', axis=0, tiled=True)]
    psum x1 -> x0, blocking collectives: 27.6 us -> none  [local(): lax.psum((in_share, out_share, filter_share, vector_share), 'dp')]
    unnamed x2 -> x0, blocking collectives: 25.4 us -> none
  transfers between devices with their start and end apart: 6 -> 0, of which waited for: 3 -> 0; matrix products, arithmetic and copies ran while one was open for 42% -> 0% of each run, Pallas kernels for 0% -> 0%
where the time goes in v1:
time: 334 us; the launch traced here: 333 us
  Pallas kernels  299 us (90%)
  matrix products  24.5 us (7%)
  local copies, waits for them, and re-layouts  6.23 us (2%)
    pallas_call x1, Pallas kernels, bwd_call(): pl.pallas_call(functools.partial(bwd_kernel, remote), grid=(blocks,), in_...  99.8 us
    pallas_call x1, Pallas kernels, project_call(): pl.pallas_call(project_kernel, grid=(CT + length // T,), in_specs=[whole(...  84.1 us
    pallas_call x1, Pallas kernels, token_call(): pl.pallas_call(functools.partial(token_kernel, remote), grid=(length // T...  64 us
    pallas_call x1, Pallas kernels, fwd_call(): pl.pallas_call(fwd_kernel, grid=(blocks,), in_specs=[wide_block, wide_blo...  30 us
    dot_general x3, matrix products, dot_tn(): lax.dot_general(a, b, (((0,), (0,)), ((), ())), preferred_element_type=F32)  24.5 us
    pallas_call x2, Pallas kernels, adam_call(): pl.pallas_call(kernel, grid=(-(-rows // tile),), in_specs=[*grad_specs, d...  21.3 us

profile of v1, /device:TPU:1, one launch (start us, length us, event | category | flops | bytes accessed | tf_op | source)
XLA Modules:
  0.0 333.0 jit_solution(16472169984610673319)
XLA Ops:
  0.6 0.7 pad.7
  1.4 0.7 reshape.77
  2.1 0.3 scatter.4.small_ref
  2.4 0.0 copy-start.3
  2.4 0.6 copy-done.3
  3.0 84.1 %shard_map.254 = (bf16[1024,2304]{1,0:T(8,128)(2,1)}, bf16[1024,2304]{1,0:T(8,128)(2,1)}, bf16[1024,2304]{1,0:T(8,128)(2,1)}, f32[1024,2048]{1,0:T(8,128)}, bf16...) custom-call(bf16[1024,1024]{1,0:T(8,128)(2,1)} %bitcast.36, ...), custom_call_target="tpu_custom_call" | custom-call | flops 4831838208 | bytes 41943040 | tf_op jit(solution)/shard_map/pallas_call | solution.py:780
  87.1 30.0 %shard_map.255 = (bf16[1024,1024]{1,0:T(8,128)(2,1)}, bf16[1024,2048]{1,0:T(8,128)(2,1)}, bf16[1024,2048]{1,0:T(8,128)(2,1)}, bf16[1024,2048]{1,0:T(8,128)(2,1)}...) custom-call(bf16[1024,2304]{1,0:T(8,128)(2,1)} %get-tuple-element.62.xs_ref.refs_0_.refs_1_, ...), custom_call_target="tpu_custom_call" | custom-call | flops 12884901888 | bytes 41943040 | tf_op jit(solution)/shard_map/pallas_call | solution.py:921
  117.2 0.0 copy-start.13
  117.2 0.0 copy-start.15
  117.2 8.5 %convolution_convert_fusion.1 = bf16[1024,2048]{1,0:T(8,128)(2,1)} fusion(bf16[1024,1024]{1,0:T(8,128)(2,1)S(1)} %copy-done.14, bf16[1024,2048]{1,0:T(8,128)(2,1)} %get-tuple-element.70.refs_0_), kind=kOutput, calls=%fused_computation.1 | convolution fusion | flops 4297064448 | bytes 10485760 | tf_op jit(solution)/shard_map/dot_general | solution.py:56
  125.7 6.2 %convolution_convert_fusion.2 = bf16[2048,1024]{1,0:T(8,128)(2,1)} fusion(bf16[1024,2048]{1,0:T(8,128)(2,1)S(1)} %copy-done.15, bf16[1,1024,1024]{2,1,0:T(8,128)(2,1)S(1)} %copy-done.13), kind=kOutput, calls=%fused_computation.2 | convolution fusion | flops 4297064448 | bytes 10485760 | tf_op jit(solution)/shard_map/dot_general | solution.py:56
  131.9 99.8 %shard_map.256 = (bf16[1024,2432]{1,0:T(8,128)(2,1)}, f32[40,2304]{1,0:T(8,128)}, f32[16,128]{1,0:T(8,128)}, bf16[512,1024]{1,0:T(8,128)(2,1)}, bf16[256,2048]{1,0:T(8,128)(2,1)}) custom-call(bf16[1024,2304]{1,0:T(8,128)(2,1)} %get-tuple-element.62.xs_ref.refs_0_.refs_1_, bf16[1024,2304]{1,0:T(8,128)(2,1)} %get-tuple-element.62.xs_ref.refs_0_.refs_1_, ...), custom_call_target="tpu_custom_call" | custom-call | flops 17179869184 | bytes 31457280 | tf_op jit(solution)/shard_map/pallas_call | solution.py:1209
  231.7 0.0 copy-start.5
  231.7 0.0 copy-start.4
  231.7 9.8 %convolution_convert_fusion = bf16[1024,2432]{1,0:T(8,128)(2,1)} fusion(bf16[1024,1024]{1,0:T(8,128)(2,1)S(1)} %copy-done.14, bf16[1024,2432]{1,0:T(8,128)(2,1)} %get-tuple-element.81.refs_1_), kind=kOutput, calls=%fused_computation | convolution fusion | flops 5102764032 | bytes 12058624 | tf_op jit(solution)/shard_map/dot_general | solution.py:56
  241.5 0.1 bitcast_reduce_fusion.refs_7_
  241.6 0.0 copy-start.2
  241.7 0.1 reshape.82
  241.8 0.1 reduce_sum.49
  242.0 0.1 concatenate.5
  242.1 0.6 broadcast_in_dim.18.refs_8_
  242.7 64.0 %shard_map.257 = (f32[1024,1024]{1,0:T(8,128)}, f32[16,1408]{1,0:T(8,128)}, bf16[256,2432]{1,0:T(8,128)(2,1)}) custom-call(bf16[1024,2048]{1,0:T(8,128)(2,1)} %get-tuple-element.70.refs_0_, bf16[1024,2432]{1,0:T(8,128)(2,1)} %get-tuple-element.81.refs_1_, bf16[1024,2048]{1,0:T(8,128)(2,1)} %get-tuple-element.65.wg_ref.refs_2_, ...), custom_call_target="tpu_custom_call" | custom-call | flops 9395240960 | bytes 23068672 | tf_op jit(solution)/shard_map/pallas_call | solution.py:1397
  306.7 0.0 copy-start.7
  306.7 0.0 copy-start.10
  306.7 0.0 copy-start.6
  306.7 0.0 copy-start.8
  306.7 14.6 %shard_map.258 = (f32[4384,256]{1,0:T(8,128)}, f32[4384,256]{1,0:T(8,128)}, f32[4384,256]{1,0:T(8,128)}) custom-call(bf16[256,2048]{1,0:T(8,128)(2,1)} %get-tuple-element.88.first_ref, bf16[256,2432]{1,0:T(8,128)(2,1)} %get-tuple-element.89.second_ref, f32[4384,256]{1,0:T(8,128)} %bitcast.29, f32[4384,256]{1,0:T(8,128)} %bitcast.30, f32[4384,256]{1,0:T(8,128)} %bitcast.31), custom_call_target="tpu_custom_call" | custom-call | bytes 29179904 | tf_op jit(solution)/shard_map/pallas_call | solution.py:1495
  321.4 1.0 slice_reduce_fusion.1
  322.4 0.6 multiply_subtract_fusion.1
  323.0 1.4 multiply_subtract_fusion
  324.4 6.6 %shard_map.259 = (f32[512,1024]{1,0:T(8,128)}, f32[512,1024]{1,0:T(8,128)}, f32[512,1024]{1,0:T(8,128)}) custom-call(bf16[512,1024]{1,0:T(8,128)(2,1)} %get-tuple-element.91.grad_ref, f32[512,1024]{1,0:T(8,128)} %refs_0_.1, f32[512,1024]{1,0:T(8,128)} %refs_1_.1, f32[512,1024]{1,0:T(8,128)} %refs_2_.1), custom_call_target="tpu_custom_call" | custom-call | bytes 13631488 | tf_op jit(solution)/shard_map/pallas_call | solution.py:1495
  331.0 2.0 copy.31
  (28 shorter events, 0.2 us)
Async XLA Ops:
  2.4 0.6 copy-start.3
  87.1 30.1 %copy-start.14 = (bf16[1024,1024]{1,0:T(8,128)(2,1)S(1)}, bf16[1024,1024]{1,0:T(8,128)(2,1)}, u32[]{:S(2)}) copy-start(bf16[1024,1024]{1,0:T(8,128)(2,1)} %get-tuple-element.64.nrm_ref) | copy-start | bytes 6291460
  117.2 8.5 %copy-start.13 = (bf16[1,1024,1024]{2,1,0:T(8,128)(2,1)S(1)}, bf16[1,1024,1024]{2,1,0:T(8,128)(2,1)}, u32[]{:S(2)}) copy-start(bf16[1,1024,1024]{2,1,0:T(8,128)(2,1)} %param.18) | copy-start | bytes 6291460
  117.2 8.5 %copy-start.15 = (bf16[1024,2048]{1,0:T(8,128)(2,1)S(1)}, bf16[1024,2048]{1,0:T(8,128)(2,1)}, u32[]{:S(2)}) copy-start(bf16[1024,2048]{1,0:T(8,128)(2,1)} %get-tuple-element.80) | copy-start | bytes 12582916
  231.7 9.9 %copy-start.1 = (f32[40,2304]{1,0:T(8,128)S(1)}, f32[40,2304]{1,0:T(8,128)}, u32[]{:S(2)}) copy-start(f32[40,2304]{1,0:T(8,128)} %get-tuple-element.83) | copy-start | bytes 1105924
  231.7 10.0 %copy-start.12 = (f32[16,128]{1,0:T(8,128)S(1)}, f32[16,128]{1,0:T(8,128)}, u32[]{:S(2)}) copy-start(f32[16,128]{1,0:T(8,128)} %get-tuple-element.85) | copy-start | bytes 24580
  231.7 10.0 %copy-start.5 = (f32[8,2048]{1,0:T(8,128)S(1)}, f32[8,2048]{1,0:T(8,128)}, u32[]{:S(2)}) copy-start(f32[8,2048]{1,0:T(8,128)} %get-tuple-element.86) | copy-start | bytes 196612
  231.7 10.2 %copy-start.4 = (f32[8,2048]{1,0:T(8,128)S(1)}, f32[8,2048]{1,0:T(8,128)}, u32[]{:S(2)}) copy-start(f32[8,2048]{1,0:T(8,128)} %get-tuple-element.84) | copy-start | bytes 196612
  241.6 1.1 copy-start.2
  306.7 15.7 %copy-start.7 = (f32[1368]{0:T(1024)S(1)}, f32[1368]{0:T(1024)}, u32[]{:S(2)}) copy-start(f32[1368]{0:T(1024)} %param.23) | copy-start | bytes 16420
  306.7 15.7 %copy-start.10 = (f32[1368]{0:T(1024)S(1)}, f32[1368]{0:T(1024)}, u32[]{:S(2)}) copy-start(f32[1368]{0:T(1024)} %param.27) | copy-start | bytes 16420
  306.7 15.7 %copy-start.11 = (f32[1368]{0:T(1024)S(1)}, f32[1368]{0:T(1024)}, u32[]{:S(2)}) copy-start(f32[1368]{0:T(1024)} %param.31) | copy-start | bytes 16420
  306.7 16.3 %copy-start.6 = (f32[4,576]{1,0:T(4,128)S(1)}, f32[4,576]{1,0:T(4,128)}, u32[]{:S(2)}) copy-start(f32[4,576]{1,0:T(4,128)} %param.22) | copy-start | bytes 27652
  306.7 16.3 %copy-start.8 = (f32[4,576]{1,0:T(4,128)S(1)}, f32[4,576]{1,0:T(4,128)}, u32[]{:S(2)}) copy-start(f32[4,576]{1,0:T(4,128)} %param.26) | copy-start | bytes 27652
  306.7 16.3 %copy-start.9 = (f32[4,576]{1,0:T(4,128)S(1)}, f32[4,576]{1,0:T(4,128)}, u32[]{:S(2)}) copy-start(f32[4,576]{1,0:T(4,128)} %param.30) | copy-start | bytes 27652
  321.4 9.6 %copy-start = (f32[1024,1024]{1,0:T(8,128)S(1)}, f32[1024,1024]{1,0:T(8,128)}, u32[]{:S(2)}) copy-start(f32[1024,1024]{1,0:T(8,128)} %get-tuple-element.87) | copy-start | bytes 12582916

commit v2 on v1

--- a/solution.py
+++ b/solution.py
@@ -99,6 +99,31 @@
     pl.semaphore_wait(barrier, len(hops))
 
 
+class Transfer:
+    def __init__(self, hop, src, dst, send, recv, ways):
+        rows = src.shape[-2]
+        lead = (slice(None),) * (len(src.shape) - 2)
+        parts = [(*lead, pl.ds(i * rows // ways, rows // ways)) for i in range(ways)]
+
+        def copy(a, b):
+            return pltpu.make_async_remote_copy(
+                src_ref=a, dst_ref=b, send_sem=send, recv_sem=recv, device_id=across(hop), device_id_type=MESH
+            )
+
+        self.parts = [copy(src.at[at], dst.at[at]) for at in parts] if ways > 1 else [copy(src, dst)]
+        self.whole = copy(src, dst)
+
+    def start(self):
+        for part in self.parts:
+            part.start()
+
+    def wait_recv(self):
+        self.whole.wait_recv()
+
+    def wait_send(self):
+        self.whole.wait_send()
+
+
 def rows_at(start, size):
     return pl.ds(pl.multiple_of(start, size), size)
 
@@ -117,11 +142,8 @@
     base1 = base + z1 * quarter
     base2 = base1 + z2 * eighth
 
-    def copy(n, hop, a, b):
-        return pltpu.make_async_remote_copy(
-            src_ref=a, dst_ref=b, send_sem=sends.at[index, n], recv_sem=recvs.at[index, n],
-            device_id=across(hop), device_id_type=MESH,
-        )
+    def copy(n, hop, a, b, ways=1):
+        return Transfer(hop, a, b, sends.at[index, n], recvs.at[index, n], ways)
 
     def pair(u):
         return own.at[:, u] if first_x else own.at[u]
@@ -130,14 +152,14 @@
     load = pltpu.make_async_copy(src.at[:, :, rows_at(base, half), cols], own, local_sem)
     here = [total.at[rows_at(base2, eighth)], total.at[rows_at(base1, quarter)], total.at[rows_at(base, half)]]
     copies = [
-        copy(0, CORE, src.at[:, :, rows_at((1 - c) * half, half), cols], r0),
-        copy(1, first, pair(1 - kept), r1),
-        copy(2, second, r1.at[1 - bit(second)], r2),
-        copy(3, Z_NEAR, r2.at[rows_at((1 - z1) * quarter, quarter)], r3),
+        copy(0, CORE, src.at[:, :, rows_at((1 - c) * half, half), cols], r0, 4),
+        copy(1, first, pair(1 - kept), r1, 4),
+        copy(2, second, r1.at[1 - bit(second)], r2, 4),
+        copy(3, Z_NEAR, r2.at[rows_at((1 - z1) * quarter, quarter)], r3, 2),
         copy(4, Z_FAR, r3.at[rows_at((1 - z2) * eighth, eighth)], r4),
         copy(5, Z_FAR, here[0], here[0]),
-        copy(6, Z_NEAR, here[1], here[1]),
-        copy(7, CORE, here[2], here[2]),
+        copy(6, Z_NEAR, here[1], here[1], 2),
+        copy(7, CORE, here[2], here[2], 2),
     ]
 
     def begin():
@@ -381,33 +403,37 @@
     st_ref[0] = state[...].astype(BF16)
     carr_scr[...] = dot_nn(cmat, st_ref[0])
 
-    def group(i, _):
-        cols = tile_at(i)
+    def here(rows):
+        return pl.ds(pl.multiple_of(block * T + rows.start, CHUNK), CHUNK)
+
+    def prepare(i, p):
+        cols = tile_of(i)
         for rows in chunks():
-            here = pl.ds(pl.multiple_of(block * T + rows.start, CHUNK), CHUNK)
-            x1 = (act[here, cols].astype(F32) * step_f[rows, cols]).astype(BF16)
-            put_diagonal(diag, rows.start, x1)
+            x1 = (act[here(rows), cols].astype(F32) * step_f[rows, cols]).astype(BF16)
+            put_diagonal(diag.at[p], rows.start, x1)
             xw_scr[rows, cols] = (x1.astype(F32) * to_end[rows, cols]).astype(BF16)
         for k in range(HPT):
-            row = cum_rows[pl.ds(HPT * i + k, 1), :]
+            row = cum_rows[HPT * i + k : HPT * i + k + 1, :]
             for rows in chunks():
                 n = LANES if rows.start < LANES else T
                 colb = cum_b[HPT * i + k, rows]
                 colb = colb if n == LANES else wide(colb)
                 decay = jnp.exp2(jnp.minimum(colb - row[:, :n], 0.0)).astype(BF16)
-                wcat[rows, k * T : k * T + n] = scores[rows, :n] * decay
-        y_ref[:, cols] = dot_nn(wcat[...], diag[...])
+                wcat[p, rows, k * T : k * T + n] = scores[rows, :n] * decay
+
+    prepare(0, 0)
+    for i in range(NT):
+        cols = tile_of(i)
+        y_ref[:, cols] = dot_nn(wcat[i % 2], diag[i % 2])
+        if i + 1 < NT:
+            prepare(i + 1, (i + 1) % 2)
         skip = skip_ref[0:1, cols]
         for rows in chunks():
-            here = pl.ds(pl.multiple_of(block * T + rows.start, CHUNK), CHUNK)
             y = y_ref[rows, cols] + carr_scr[rows, cols] * from_start[rows, cols]
-            y_ref[rows, cols] = y + act[here, cols].astype(F32) * skip
+            y_ref[rows, cols] = y + act[here(rows), cols].astype(F32) * skip
         fade = from_start_last(cum_b, i) * keep
         for rows in chunks(0, NSTATE):
             state[rows, cols] = state[rows, cols] * fade
-        return 0
-
-    lax.fori_loop(0, NT, group, 0)
     state[...] += dot_nn(b_t, xw_scr[...])
 
 
@@ -416,11 +442,11 @@
         pltpu.VMEM((NSTATE, D_INNER), F32),
         pltpu.VMEM((H, T, LANES), F32),
         pltpu.VMEM((2 * LANES, D_INNER), BF16),
-        pltpu.VMEM((T, HPT * T), BF16),
+        pltpu.VMEM((2, T, HPT * T), BF16),
         pltpu.VMEM((LANES, T), F32),
         pltpu.VMEM((T, D_INNER), BF16),
         pltpu.VMEM((T, D_INNER), F32),
-        pltpu.VMEM((HPT * T, W), BF16),
+        pltpu.VMEM((2, HPT * T, W), BF16),
         pltpu.VMEM((T, T), BF16),
         pltpu.VMEM((8, LANES), F32),
         pltpu.VMEM((T, D_INNER), F32),
@@ -476,8 +502,13 @@
     cols = tile_at(j)
     taps = [taps_ref[k : k + 1, cols] for k in range(KERNEL)]
     bias = vec_ref[0:1, pl.ds(pl.multiple_of(D + D_INNER + j * W, W), W)]
+    def product(top):
+        pad[8 + top : 8 + top + T] = dot_nn(nrm_ref[top : top + T], w[:, cols])
+
+    product(0)
     for top in range(0, length, T):
-        pad[8 + top : 8 + top + T] = dot_nn(nrm_ref[top : top + T], w[:, cols])
+        if top + T < length:
+            product(top + T)
         for r in range(top, top + T, CHUNK):
             here = pad[8 + r : 8 + r + CHUNK]
             cin_ref[r : r + CHUNK] = here.astype(BF16)
@@ -500,10 +531,7 @@
     top = bit(CORE) * half
 
     def copy(n, a, b, hop):
-        return pltpu.make_async_remote_copy(
-            src_ref=a, dst_ref=b, send_sem=sends.at[index, n], recv_sem=recvs.at[index, n],
-            device_id=across(hop), device_id_type=MESH,
-        )
+        return Transfer(hop, a, b, sends.at[index, n], recvs.at[index, n], 2)
 
     def onward(n, slot, start, size, hop):
         return copy(n, put(slot * rows + start, size), put(slot * rows + start, size), hop)

time: 334 us -> 332 us (level)
    pallas_call x1, Pallas kernels: 84.1 us -> 78.4 us  [project_call(): pl.pallas_call(project_kernel, grid=(CT + length // T,), in_specs=[whole(...]
where the time goes in v2:
time: 332 us; the launch traced here: 331 us
  Pallas kernels  297 us (89%)
  matrix products  24.5 us (7%)
  local copies, waits for them, and re-layouts  6.23 us (2%)
    pallas_call x1, Pallas kernels, bwd_call(): pl.pallas_call(functools.partial(bwd_kernel, remote), grid=(blocks,), in_...  103 us
    pallas_call x1, Pallas kernels, project_call(): pl.pallas_call(project_kernel, grid=(CT + length // T,), in_specs=[whole(...  78.4 us
    pallas_call x1, Pallas kernels, token_call(): pl.pallas_call(functools.partial(token_kernel, remote), grid=(length // T...  64.7 us
    pallas_call x1, Pallas kernels, fwd_call(): pl.pallas_call(fwd_kernel, grid=(blocks,), in_specs=[wide_block, wide_blo...  30 us
    dot_general x3, matrix products, dot_tn(): lax.dot_general(a, b, (((0,), (0,)), ((), ())), preferred_element_type=F32)  24.5 us
    pallas_call x2, Pallas kernels, adam_call(): pl.pallas_call(kernel, grid=(-(-rows // tile),), in_specs=[*grad_specs, d...  21.3 us

profile of v2, /device:TPU:1, one launch (start us, length us, event | category | flops | bytes accessed | tf_op | source)
XLA Modules:
  0.0 331.3 jit_solution(2891837708290047464)
XLA Ops:
  0.6 0.7 pad.7
  1.4 0.7 reshape.77
  2.1 0.3 scatter.4.small_ref
  2.4 0.0 copy-start.3
  2.4 0.6 copy-done.3
  3.0 78.4 %shard_map.254 = (bf16[1024,2304]{1,0:T(8,128)(2,1)}, bf16[1024,2304]{1,0:T(8,128)(2,1)}, bf16[1024,2304]{1,0:T(8,128)(2,1)}, f32[1024,2048]{1,0:T(8,128)}, bf16...) custom-call(bf16[1024,1024]{1,0:T(8,128)(2,1)} %bitcast.36, ...), custom_call_target="tpu_custom_call" | custom-call | flops 4831838208 | bytes 41943040 | tf_op jit(solution)/shard_map/pallas_call | solution.py:808
  81.5 30.0 %shard_map.255 = (bf16[1024,1024]{1,0:T(8,128)(2,1)}, bf16[1024,2048]{1,0:T(8,128)(2,1)}, bf16[1024,2048]{1,0:T(8,128)(2,1)}, bf16[1024,2048]{1,0:T(8,128)(2,1)}...) custom-call(bf16[1024,2304]{1,0:T(8,128)(2,1)} %get-tuple-element.62.xs_ref.refs_0_.refs_1_, ...), custom_call_target="tpu_custom_call" | custom-call | flops 12884901888 | bytes 41943040 | tf_op jit(solution)/shard_map/pallas_call | solution.py:949
  111.5 0.0 copy-start.13
  111.5 0.0 copy-start.15
  111.6 8.5 %convolution_convert_fusion.1 = bf16[1024,2048]{1,0:T(8,128)(2,1)} fusion(bf16[1024,1024]{1,0:T(8,128)(2,1)S(1)} %copy-done.14, bf16[1024,2048]{1,0:T(8,128)(2,1)} %get-tuple-element.70.refs_0_), kind=kOutput, calls=%fused_computation.1 | convolution fusion | flops 4297064448 | bytes 10485760 | tf_op jit(solution)/shard_map/dot_general | solution.py:56
  120.0 6.2 %convolution_convert_fusion.2 = bf16[2048,1024]{1,0:T(8,128)(2,1)} fusion(bf16[1024,2048]{1,0:T(8,128)(2,1)S(1)} %copy-done.15, bf16[1,1024,1024]{2,1,0:T(8,128)(2,1)S(1)} %copy-done.13), kind=kOutput, calls=%fused_computation.2 | convolution fusion | flops 4297064448 | bytes 10485760 | tf_op jit(solution)/shard_map/dot_general | solution.py:56
  126.2 102.9 %shard_map.256 = (bf16[1024,2432]{1,0:T(8,128)(2,1)}, f32[40,2304]{1,0:T(8,128)}, f32[16,128]{1,0:T(8,128)}, bf16[512,1024]{1,0:T(8,128)(2,1)}, bf16[256,2048]{1,0:T(8,128)(2,1)}) custom-call(bf16[1024,2304]{1,0:T(8,128)(2,1)} %get-tuple-element.62.xs_ref.refs_0_.refs_1_, bf16[1024,2304]{1,0:T(8,128)(2,1)} %get-tuple-element.62.xs_ref.refs_0_.refs_1_, ...), custom_call_target="tpu_custom_call" | custom-call | flops 17179869184 | bytes 31457280 | tf_op jit(solution)/shard_map/pallas_call | solution.py:1237
  229.2 0.0 copy-start.5
  229.2 0.0 copy-start.4
  229.2 9.8 %convolution_convert_fusion = bf16[1024,2432]{1,0:T(8,128)(2,1)} fusion(bf16[1024,1024]{1,0:T(8,128)(2,1)S(1)} %copy-done.14, bf16[1024,2432]{1,0:T(8,128)(2,1)} %get-tuple-element.81.refs_1_), kind=kOutput, calls=%fused_computation | convolution fusion | flops 5102764032 | bytes 12058624 | tf_op jit(solution)/shard_map/dot_general | solution.py:56
  239.0 0.1 bitcast_reduce_fusion.refs_7_
  239.1 0.0 copy-start.2
  239.2 0.1 reshape.82
  239.3 0.1 reduce_sum.49
  239.5 0.1 concatenate.5
  239.6 0.6 broadcast_in_dim.18.refs_8_
  240.2 64.7 %shard_map.257 = (f32[1024,1024]{1,0:T(8,128)}, f32[16,1408]{1,0:T(8,128)}, bf16[256,2432]{1,0:T(8,128)(2,1)}) custom-call(bf16[1024,2048]{1,0:T(8,128)(2,1)} %get-tuple-element.70.refs_0_, bf16[1024,2432]{1,0:T(8,128)(2,1)} %get-tuple-element.81.refs_1_, bf16[1024,2048]{1,0:T(8,128)(2,1)} %get-tuple-element.65.wg_ref.refs_2_, ...), custom_call_target="tpu_custom_call" | custom-call | flops 9395240960 | bytes 23068672 | tf_op jit(solution)/shard_map/pallas_call | solution.py:1425
  304.9 0.0 copy-start.7
  304.9 0.0 copy-start.10
  305.0 0.0 copy-start.8
  305.0 0.0 copy-start.9
  305.0 14.6 %shard_map.258 = (f32[4384,256]{1,0:T(8,128)}, f32[4384,256]{1,0:T(8,128)}, f32[4384,256]{1,0:T(8,128)}) custom-call(bf16[256,2048]{1,0:T(8,128)(2,1)} %get-tuple-element.88.first_ref, bf16[256,2432]{1,0:T(8,128)(2,1)} %get-tuple-element.89.second_ref, f32[4384,256]{1,0:T(8,128)} %bitcast.29, f32[4384,256]{1,0:T(8,128)} %bitcast.30, f32[4384,256]{1,0:T(8,128)} %bitcast.31), custom_call_target="tpu_custom_call" | custom-call | bytes 29179904 | tf_op jit(solution)/shard_map/pallas_call | solution.py:1523
  319.6 1.0 slice_reduce_fusion.1
  320.6 0.6 multiply_subtract_fusion.1
  321.3 1.4 multiply_subtract_fusion
  322.6 6.6 %shard_map.259 = (f32[512,1024]{1,0:T(8,128)}, f32[512,1024]{1,0:T(8,128)}, f32[512,1024]{1,0:T(8,128)}) custom-call(bf16[512,1024]{1,0:T(8,128)(2,1)} %get-tuple-element.91.grad_ref, f32[512,1024]{1,0:T(8,128)} %refs_0_.1, f32[512,1024]{1,0:T(8,128)} %refs_1_.1, f32[512,1024]{1,0:T(8,128)} %refs_2_.1), custom_call_target="tpu_custom_call" | custom-call | bytes 13631488 | tf_op jit(solution)/shard_map/pallas_call | solution.py:1523
  329.2 2.0 copy.31
  (28 shorter events, 0.2 us)
Async XLA Ops:
  2.4 0.6 copy-start.3
  81.5 30.1 %copy-start.14 = (bf16[1024,1024]{1,0:T(8,128)(2,1)S(1)}, bf16[1024,1024]{1,0:T(8,128)(2,1)}, u32[]{:S(2)}) copy-start(bf16[1024,1024]{1,0:T(8,128)(2,1)} %get-tuple-element.64.nrm_ref) | copy-start | bytes 6291460
  111.5 8.5 %copy-start.13 = (bf16[1,1024,1024]{2,1,0:T(8,128)(2,1)S(1)}, bf16[1,1024,1024]{2,1,0:T(8,128)(2,1)}, u32[]{:S(2)}) copy-start(bf16[1,1024,1024]{2,1,0:T(8,128)(2,1)} %param.18) | copy-start | bytes 6291460
  111.5 8.5 %copy-start.15 = (bf16[1024,2048]{1,0:T(8,128)(2,1)S(1)}, bf16[1024,2048]{1,0:T(8,128)(2,1)}, u32[]{:S(2)}) copy-start(bf16[1024,2048]{1,0:T(8,128)(2,1)} %get-tuple-element.80) | copy-start | bytes 12582916
  229.2 9.9 %copy-start.1 = (f32[40,2304]{1,0:T(8,128)S(1)}, f32[40,2304]{1,0:T(8,128)}, u32[]{:S(2)}) copy-start(f32[40,2304]{1,0:T(8,128)} %get-tuple-element.83) | copy-start | bytes 1105924
  229.2 10.0 %copy-start.12 = (f32[16,128]{1,0:T(8,128)S(1)}, f32[16,128]{1,0:T(8,128)}, u32[]{:S(2)}) copy-start(f32[16,128]{1,0:T(8,128)} %get-tuple-element.85) | copy-start | bytes 24580
  229.2 10.0 %copy-start.5 = (f32[8,2048]{1,0:T(8,128)S(1)}, f32[8,2048]{1,0:T(8,128)}, u32[]{:S(2)}) copy-start(f32[8,2048]{1,0:T(8,128)} %get-tuple-element.86) | copy-start | bytes 196612
  229.2 10.2 %copy-start.4 = (f32[8,2048]{1,0:T(8,128)S(1)}, f32[8,2048]{1,0:T(8,128)}, u32[]{:S(2)}) copy-start(f32[8,2048]{1,0:T(8,128)} %get-tuple-element.84) | copy-start | bytes 196612
  239.1 1.1 copy-start.2
  304.9 15.7 %copy-start.7 = (f32[1368]{0:T(1024)S(1)}, f32[1368]{0:T(1024)}, u32[]{:S(2)}) copy-start(f32[1368]{0:T(1024)} %param.23) | copy-start | bytes 16420
  304.9 15.7 %copy-start.10 = (f32[1368]{0:T(1024)S(1)}, f32[1368]{0:T(1024)}, u32[]{:S(2)}) copy-start(f32[1368]{0:T(1024)} %param.27) | copy-start | bytes 16420
  304.9 15.7 %copy-start.11 = (f32[1368]{0:T(1024)S(1)}, f32[1368]{0:T(1024)}, u32[]{:S(2)}) copy-start(f32[1368]{0:T(1024)} %param.31) | copy-start | bytes 16420
  304.9 16.3 %copy-start.6 = (f32[4,576]{1,0:T(4,128)S(1)}, f32[4,576]{1,0:T(4,128)}, u32[]{:S(2)}) copy-start(f32[4,576]{1,0:T(4,128)} %param.22) | copy-start | bytes 27652
  305.0 16.3 %copy-start.8 = (f32[4,576]{1,0:T(4,128)S(1)}, f32[4,576]{1,0:T(4,128)}, u32[]{:S(2)}) copy-start(f32[4,576]{1,0:T(4,128)} %param.26) | copy-start | bytes 27652
  305.0 16.3 %copy-start.9 = (f32[4,576]{1,0:T(4,128)S(1)}, f32[4,576]{1,0:T(4,128)}, u32[]{:S(2)}) copy-start(f32[4,576]{1,0:T(4,128)} %param.30) | copy-start | bytes 27652
  319.6 9.6 %copy-start = (f32[1024,1024]{1,0:T(8,128)S(1)}, f32[1024,1024]{1,0:T(8,128)}, u32[]{:S(2)}) copy-start(f32[1024,1024]{1,0:T(8,128)} %get-tuple-element.87) | copy-start | bytes 12582916

commit v3 on v2

--- a/solution.py
+++ b/solution.py
@@ -1,4 +1,5 @@
 import functools
+import itertools
 import math
 
 import jax
@@ -129,7 +130,12 @@
 
 
 def add_rows(out, a, b):
-    out[...] = a[...] + b[...]
+    *lead, rows, cols = out.shape
+    size = min(rows, max(16, 8192 // cols))
+    for at in itertools.product(*(range(n) for n in lead)):
+        for r in range(0, rows, size):
+            here = (*at, slice(r, r + size))
+            out[here] = a[here] + b[here]
 
 
 def reduce_chunk(src, cols, first_x, bufs, total, sends, recvs, index, local_sem):
@@ -152,14 +158,14 @@
     load = pltpu.make_async_copy(src.at[:, :, rows_at(base, half), cols], own, local_sem)
     here = [total.at[rows_at(base2, eighth)], total.at[rows_at(base1, quarter)], total.at[rows_at(base, half)]]
     copies = [
-        copy(0, CORE, src.at[:, :, rows_at((1 - c) * half, half), cols], r0, 4),
-        copy(1, first, pair(1 - kept), r1, 4),
-        copy(2, second, r1.at[1 - bit(second)], r2, 4),
-        copy(3, Z_NEAR, r2.at[rows_at((1 - z1) * quarter, quarter)], r3, 2),
+        copy(0, CORE, src.at[:, :, rows_at((1 - c) * half, half), cols], r0),
+        copy(1, first, pair(1 - kept), r1),
+        copy(2, second, r1.at[1 - bit(second)], r2),
+        copy(3, Z_NEAR, r2.at[rows_at((1 - z1) * quarter, quarter)], r3),
         copy(4, Z_FAR, r3.at[rows_at((1 - z2) * eighth, eighth)], r4),
         copy(5, Z_FAR, here[0], here[0]),
-        copy(6, Z_NEAR, here[1], here[1], 2),
-        copy(7, CORE, here[2], here[2], 2),
+        copy(6, Z_NEAR, here[1], here[1]),
+        copy(7, CORE, here[2], here[2]),
     ]
 
     def begin():
@@ -1471,38 +1477,44 @@
     )(gg, gc, wg, wc, tok, cot, vec, taps_sum, vec_sum, *((grad_conv,) if remote else ()))
 
 
+FIRST_FIX = 1.0 / (1.0 - BETA_FIRST**STEP)
+SECOND_FIX = 1.0 / (1.0 - BETA_SECOND**STEP)
+
+
 def adam_step(master, first, second, grad, rate):
     first_new = BETA_FIRST * first + (1.0 - BETA_FIRST) * grad
     second_new = BETA_SECOND * second + (1.0 - BETA_SECOND) * grad * grad
-    first_fix = 1.0 - BETA_FIRST**STEP
-    second_fix = 1.0 - BETA_SECOND**STEP
-    master_new = master - rate * (
-        first_new / first_fix / (jnp.sqrt(second_new / second_fix) + ADAM_EPSILON) + WEIGHT_DECAY * master
-    )
-    return (master_new, first_new, second_new)
-
-
-def adam_rows(rate, grad, refs, rows):
+    step = (rate * FIRST_FIX) * first_new / (jnp.sqrt(second_new * SECOND_FIX) + ADAM_EPSILON)
+    return ((1.0 - rate * WEIGHT_DECAY) * master - step, first_new, second_new)
+
+
+def adam_rows(rate, grad, refs, at):
     ins, outs = refs
-    for ref, value in zip(outs, adam_step(*(r[rows] for r in ins), grad, rate)):
-        ref[rows] = value
+    for ref, value in zip(outs, adam_step(*(r[at] for r in ins), grad, rate)):
+        ref[at] = value
 
 
 def adam_turned_kernel(rate, tiles, first_ref, second_ref, *refs):
+    *refs, turned = refs
     j = pl.program_id(0)
     for which, grad_ref in enumerate((first_ref, second_ref)):
 
         @pl.when((j >= tiles) == bool(which))
         def _():
             for r in range(0, 2 * W, LANES):
-                rows = slice(r, r + LANES)
-                adam_rows(rate, grad_ref[:, rows].astype(F32).T, (refs[:3], refs[3:]), rows)
+                turned[r : r + LANES] = grad_ref[:, r : r + LANES].astype(F32).T
+
+    for r in range(0, 2 * W, CHUNK):
+        at = slice(r, r + CHUNK)
+        adam_rows(rate, turned[at], (refs[:3], refs[3:]), at)
 
 
 def adam_kernel(rate, grad_ref, *refs):
-    for r in range(0, refs[0].shape[0], 32):
-        rows = slice(r, r + 32)
-        adam_rows(rate, grad_ref[rows].astype(F32), (refs[:3], refs[3:]), rows)
+    rows, cols = refs[0].shape
+    for r in range(0, rows, CHUNK):
+        for c in range(0, cols, W):
+            at = (slice(r, r + CHUNK), slice(c, c + W))
+            adam_rows(rate, grad_ref[at].astype(F32), (refs[:3], refs[3:]), at)
 
 
 def adam_call(grads, master, first, second, rate):
@@ -1520,12 +1532,14 @@
         kernel = functools.partial(adam_kernel, rate)
         grad_specs = [pl.BlockSpec((tile, cols), lambda j: (j, 0))]
     down = pl.BlockSpec((tile, cols), lambda j: (j, 0))
+    scratch = [pltpu.VMEM((tile, cols), F32)] if len(grads) == 2 else []
     return pl.pallas_call(
         kernel,
         grid=(-(-rows // tile),),
         in_specs=[*grad_specs, down, down, down],
         out_specs=[down] * 3,
         out_shape=[jax.ShapeDtypeStruct((rows, cols), F32)] * 3,
+        scratch_shapes=scratch,
         compiler_params=pltpu.CompilerParams(vmem_limit_bytes=VMEM_LIMIT),
         cost_estimate=pl.CostEstimate(flops=0, bytes_accessed=26 * rows * cols, transcendentals=0),
     )(*grads, master, first, second)

time: 332 us -> 330 us (level)
  no operation moved by 1% of the time
where the time goes in v3:
time: 330 us
  Pallas kernels  296 us (90%)
  matrix products  24.5 us (7%)
  local copies, waits for them, and re-layouts  6.23 us (2%)
    pallas_call x1, Pallas kernels, bwd_call(): pl.pallas_call(functools.partial(bwd_kernel, remote), grid=(blocks,), in_...  102 us
    pallas_call x1, Pallas kernels, project_call(): pl.pallas_call(project_kernel, grid=(CT + length // T,), in_specs=[whole(...  78.4 us
    pallas_call x1, Pallas kernels, token_call(): pl.pallas_call(functools.partial(token_kernel, remote), grid=(length // T...  64.7 us
    pallas_call x1, Pallas kernels, fwd_call(): pl.pallas_call(fwd_kernel, grid=(blocks,), in_specs=[wide_block, wide_blo...  30 us
    dot_general x3, matrix products, dot_tn(): lax.dot_general(a, b, (((0,), (0,)), ((), ())), preferred_element_type=F32)  24.5 us
    pallas_call x2, Pallas kernels, adam_call(): pl.pallas_call(kernel, grid=(-(-rows // tile),), in_specs=[*grad_specs, d...  20.8 us

profile of v3, /device:TPU:1, one launch (start us, length us, event | category | flops | bytes accessed | tf_op | source)
XLA Modules:
  0.0 329.7 jit_solution(8893689120308871722)
XLA Ops:
  0.6 0.7 pad.7
  1.4 0.7 reshape.77
  2.1 0.3 scatter.4.small_ref
  2.4 0.0 copy-start.3
  2.4 0.6 copy-done.3
  3.0 78.4 %shard_map.254 = (bf16[1024,2304]{1,0:T(8,128)(2,1)}, bf16[1024,2304]{1,0:T(8,128)(2,1)}, bf16[1024,2304]{1,0:T(8,128)(2,1)}, f32[1024,2048]{1,0:T(8,128)}, bf16...) custom-call(bf16[1024,1024]{1,0:T(8,128)(2,1)} %bitcast.36, ...), custom_call_target="tpu_custom_call" | custom-call | flops 4831838208 | bytes 41943040 | tf_op jit(solution)/shard_map/pallas_call | solution.py:814
  81.5 30.0 %shard_map.255 = (bf16[1024,1024]{1,0:T(8,128)(2,1)}, bf16[1024,2048]{1,0:T(8,128)(2,1)}, bf16[1024,2048]{1,0:T(8,128)(2,1)}, bf16[1024,2048]{1,0:T(8,128)(2,1)}...) custom-call(bf16[1024,2304]{1,0:T(8,128)(2,1)} %get-tuple-element.62.xs_ref.refs_0_.refs_1_, ...), custom_call_target="tpu_custom_call" | custom-call | flops 12884901888 | bytes 41943040 | tf_op jit(solution)/shard_map/pallas_call | solution.py:955
  111.5 0.0 copy-start.13
  111.5 0.0 copy-start.15
  111.6 8.5 %convolution_convert_fusion.1 = bf16[1024,2048]{1,0:T(8,128)(2,1)} fusion(bf16[1024,1024]{1,0:T(8,128)(2,1)S(1)} %copy-done.14, bf16[1024,2048]{1,0:T(8,128)(2,1)} %get-tuple-element.70.refs_0_), kind=kOutput, calls=%fused_computation.1 | convolution fusion | flops 4297064448 | bytes 10485760 | tf_op jit(solution)/shard_map/dot_general | solution.py:57
  120.0 6.2 %convolution_convert_fusion.2 = bf16[2048,1024]{1,0:T(8,128)(2,1)} fusion(bf16[1024,2048]{1,0:T(8,128)(2,1)S(1)} %copy-done.15, bf16[1,1024,1024]{2,1,0:T(8,128)(2,1)S(1)} %copy-done.13), kind=kOutput, calls=%fused_computation.2 | convolution fusion | flops 4297064448 | bytes 10485760 | tf_op jit(solution)/shard_map/dot_general | solution.py:57
  126.2 101.9 %shard_map.256 = (bf16[1024,2432]{1,0:T(8,128)(2,1)}, f32[40,2304]{1,0:T(8,128)}, f32[16,128]{1,0:T(8,128)}, bf16[512,1024]{1,0:T(8,128)(2,1)}, bf16[256,2048]{1,0:T(8,128)(2,1)}) custom-call(bf16[1024,2304]{1,0:T(8,128)(2,1)} %get-tuple-element.62.xs_ref.refs_0_.refs_1_, bf16[1024,2304]{1,0:T(8,128)(2,1)} %get-tuple-element.62.xs_ref.refs_0_.refs_1_, ...), custom_call_target="tpu_custom_call" | custom-call | flops 17179869184 | bytes 31457280 | tf_op jit(solution)/shard_map/pallas_call | solution.py:1243
  228.2 0.0 copy-start.5
  228.2 0.0 copy-start.4
  228.2 9.8 %convolution_convert_fusion = bf16[1024,2432]{1,0:T(8,128)(2,1)} fusion(bf16[1024,1024]{1,0:T(8,128)(2,1)S(1)} %copy-done.14, bf16[1024,2432]{1,0:T(8,128)(2,1)} %get-tuple-element.81.refs_1_), kind=kOutput, calls=%fused_computation | convolution fusion | flops 5102764032 | bytes 12058624 | tf_op jit(solution)/shard_map/dot_general | solution.py:57
  238.0 0.1 bitcast_reduce_fusion.refs_7_
  238.1 0.0 copy-start.2
  238.2 0.1 reshape.82
  238.3 0.1 reduce_sum.49
  238.5 0.1 concatenate.5
  238.6 0.6 broadcast_in_dim.18.refs_8_
  239.2 64.7 %shard_map.257 = (f32[1024,1024]{1,0:T(8,128)}, f32[16,1408]{1,0:T(8,128)}, bf16[256,2432]{1,0:T(8,128)(2,1)}) custom-call(bf16[1024,2048]{1,0:T(8,128)(2,1)} %get-tuple-element.70.refs_0_, bf16[1024,2432]{1,0:T(8,128)(2,1)} %get-tuple-element.81.refs_1_, bf16[1024,2048]{1,0:T(8,128)(2,1)} %get-tuple-element.65.wg_ref.refs_2_, ...), custom_call_target="tpu_custom_call" | custom-call | flops 9395240960 | bytes 23068672 | tf_op jit(solution)/shard_map/pallas_call | solution.py:1431
  303.9 0.0 copy-start.7
  303.9 0.0 copy-start.10
  303.9 0.0 copy-start.6
  303.9 0.0 copy-start.8
  303.9 14.7 %shard_map.258 = (f32[4384,256]{1,0:T(8,128)}, f32[4384,256]{1,0:T(8,128)}, f32[4384,256]{1,0:T(8,128)}) custom-call(bf16[256,2048]{1,0:T(8,128)(2,1)} %get-tuple-element.88.first_ref, bf16[256,2432]{1,0:T(8,128)(2,1)} %get-tuple-element.89.second_ref, f32[4384,256]{1,0:T(8,128)} %bitcast.29, f32[4384,256]{1,0:T(8,128)} %bitcast.30, f32[4384,256]{1,0:T(8,128)} %bitcast.31), custom_call_target="tpu_custom_call" | custom-call | bytes 29179904 | tf_op jit(solution)/shard_map/pallas_call | solution.py:1536
  318.6 1.0 slice_reduce_fusion.1
  319.6 0.6 divide_subtract_fusion.1
  320.2 1.4 divide_subtract_fusion
  321.6 6.1 %shard_map.259 = (f32[512,1024]{1,0:T(8,128)}, f32[512,1024]{1,0:T(8,128)}, f32[512,1024]{1,0:T(8,128)}) custom-call(bf16[512,1024]{1,0:T(8,128)(2,1)} %get-tuple-element.91.grad_ref, f32[512,1024]{1,0:T(8,128)} %refs_0_.1, f32[512,1024]{1,0:T(8,128)} %refs_1_.1, f32[512,1024]{1,0:T(8,128)} %refs_2_.1), custom_call_target="tpu_custom_call" | custom-call | bytes 13631488 | tf_op jit(solution)/shard_map/pallas_call | solution.py:1536
  327.7 2.0 copy.31
  (28 shorter events, 0.2 us)
Async XLA Ops:
  2.4 0.6 copy-start.3
  81.5 30.1 %copy-start.14 = (bf16[1024,1024]{1,0:T(8,128)(2,1)S(1)}, bf16[1024,1024]{1,0:T(8,128)(2,1)}, u32[]{:S(2)}) copy-start(bf16[1024,1024]{1,0:T(8,128)(2,1)} %get-tuple-element.64.nrm_ref) | copy-start | bytes 6291460
  111.5 8.5 %copy-start.13 = (bf16[1,1024,1024]{2,1,0:T(8,128)(2,1)S(1)}, bf16[1,1024,1024]{2,1,0:T(8,128)(2,1)}, u32[]{:S(2)}) copy-start(bf16[1,1024,1024]{2,1,0:T(8,128)(2,1)} %param.18) | copy-start | bytes 6291460
  111.5 8.5 %copy-start.15 = (bf16[1024,2048]{1,0:T(8,128)(2,1)S(1)}, bf16[1024,2048]{1,0:T(8,128)(2,1)}, u32[]{:S(2)}) copy-start(bf16[1024,2048]{1,0:T(8,128)(2,1)} %get-tuple-element.80) | copy-start | bytes 12582916
  228.2 9.9 %copy-start.1 = (f32[40,2304]{1,0:T(8,128)S(1)}, f32[40,2304]{1,0:T(8,128)}, u32[]{:S(2)}) copy-start(f32[40,2304]{1,0:T(8,128)} %get-tuple-element.83) | copy-start | bytes 1105924
  228.2 10.0 %copy-start.12 = (f32[16,128]{1,0:T(8,128)S(1)}, f32[16,128]{1,0:T(8,128)}, u32[]{:S(2)}) copy-start(f32[16,128]{1,0:T(8,128)} %get-tuple-element.85) | copy-start | bytes 24580
  228.2 10.0 %copy-start.5 = (f32[8,2048]{1,0:T(8,128)S(1)}, f32[8,2048]{1,0:T(8,128)}, u32[]{:S(2)}) copy-start(f32[8,2048]{1,0:T(8,128)} %get-tuple-element.86) | copy-start | bytes 196612
  228.2 10.2 %copy-start.4 = (f32[8,2048]{1,0:T(8,128)S(1)}, f32[8,2048]{1,0:T(8,128)}, u32[]{:S(2)}) copy-start(f32[8,2048]{1,0:T(8,128)} %get-tuple-element.84) | copy-start | bytes 196612
  238.1 1.1 copy-start.2
  303.9 15.7 %copy-start.7 = (f32[1368]{0:T(1024)S(1)}, f32[1368]{0:T(1024)}, u32[]{:S(2)}) copy-start(f32[1368]{0:T(1024)} %param.23) | copy-start | bytes 16420
  303.9 15.7 %copy-start.10 = (f32[1368]{0:T(1024)S(1)}, f32[1368]{0:T(1024)}, u32[]{:S(2)}) copy-start(f32[1368]{0:T(1024)} %param.27) | copy-start | bytes 16420
  303.9 15.7 %copy-start.11 = (f32[1368]{0:T(1024)S(1)}, f32[1368]{0:T(1024)}, u32[]{:S(2)}) copy-start(f32[1368]{0:T(1024)} %param.31) | copy-start | bytes 16420
  303.9 16.3 %copy-start.6 = (f32[4,576]{1,0:T(4,128)S(1)}, f32[4,576]{1,0:T(4,128)}, u32[]{:S(2)}) copy-start(f32[4,576]{1,0:T(4,128)} %param.22) | copy-start | bytes 27652
  303.9 16.3 %copy-start.8 = (f32[4,576]{1,0:T(4,128)S(1)}, f32[4,576]{1,0:T(4,128)}, u32[]{:S(2)}) copy-start(f32[4,576]{1,0:T(4,128)} %param.26) | copy-start | bytes 27652
  303.9 16.3 %copy-start.9 = (f32[4,576]{1,0:T(4,128)S(1)}, f32[4,576]{1,0:T(4,128)}, u32[]{:S(2)}) copy-start(f32[4,576]{1,0:T(4,128)} %param.30) | copy-start | bytes 27652
  318.6 9.1 %copy-start = (f32[1024,1024]{1,0:T(8,128)S(1)}, f32[1024,1024]{1,0:T(8,128)}, u32[]{:S(2)}) copy-start(f32[1024,1024]{1,0:T(8,128)} %get-tuple-element.87) | copy-start | bytes 12582916
